TPU v7x, 32 devices: a whole 2x2x4 slice. The times are simulated.
32 devices in a mesh: users: 8 (over z, x), items: 4 (over y, core).
Axes of the slice: x: 2, y: 2, z: 4, core: 2. Of those that a mesh axis runs over, the one named last changes fastest.
Arguments:
- user_factors: bfloat16 [65536, 256], P(('users', 'items')), may hold values from -1.5 to 1.5
- item_factors: bfloat16 [1024, 256], P('items'), may hold values from -1.5 to 1.5
- block_user: int32 [32, 128], P(('users', 'items')), may hold values from 0 to 15
- block_item: int32 [32, 128], P(('users', 'items')), may hold values from 0 to 7
- counts: int32 [32], P(('users', 'items')), may hold values from 1 to 128, as said below
- ratings: bfloat16 [32, 128, 128, 128], P(('users', 'items')), may hold values from -6 to 6
- weights: bfloat16 [32, 128, 128, 128], P(('users', 'items')), may hold values from 0 to 4
Outputs:
- user_grad: float32 [65536, 256], P(('users', 'items'))
- item_grad: float32 [1024, 256], P(('users', 'items'))
Inputs may be any that keep to these rules, and one draw needn't show every extreme that they name: counts[g] live slots come first on device g; later slots are ignored; some device has exactly 128 and some device exactly 1.
All inputs are finite; a program needn't handle non-finite values.
Results may differ from a plain program's by a relative error of at most 0.0022.
Values may be sent and summed in bfloat16 or wider, within the bound.
No kernel may reach another device: no remote copies, remote signals or barrier semaphores. Data moves between devices by JAX's collectives and lax.ppermute only.
A program may use at most 64 MiB of HBM per device.

v0:
```python
import functools

import jax
import jax.numpy as jnp
from jax import lax
from jax.experimental import pallas as pl
from jax.experimental.pallas import tpu as pltpu
from jax.sharding import PartitionSpec as P

grad_scale = 0.015625
decay_rate = 0.05
AXES = ("users", "items")
UNROLL = 16
WIDE = 32
VMEM = pl.BlockSpec(memory_space=pltpu.VMEM)
SMEM = pl.BlockSpec(memory_space=pltpu.SMEM)
HBM = pl.BlockSpec(memory_space=pltpu.HBM)


def phases_of(device_total):
    bit_total = device_total.bit_length() - 1
    groups = [[0]]
    for bit in range(1, bit_total, 2):
        groups.append(list(range(bit, min(bit + 2, bit_total))))
    return groups


def place_of(index, groups):
    place = 0
    for group in groups:
        for bit in reversed(group):
            place = place * 2 + ((index >> bit) & 1)
    return place


def stage_kernel(count_ref, user_ref, rating_ref, weight_ref, factor_ref, turned_ref, held_rating_ref, held_weight_ref,
                 factor_sem, rating_sems, weight_sems):
    slots, block = held_rating_ref.shape[0], held_rating_ref.shape[1]
    chunks = (count_ref[0] + UNROLL - 1) // UNROLL

    def copies(index):
        part = pl.ds(index * UNROLL, UNROLL)
        return (
            pltpu.make_async_copy(rating_ref.at[0, part], held_rating_ref.at[part], rating_sems.at[index]),
            pltpu.make_async_copy(weight_ref.at[0, part], held_weight_ref.at[part], weight_sems.at[index]),
        )

    factor_copy = pltpu.make_async_copy(user_ref, factor_ref, factor_sem)
    factor_copy.start()
    for index in range(slots // UNROLL):
        @pl.when(index < chunks)
        def _():
            for copy in copies(index):
                copy.start()
    factor_copy.wait()
    for index in range(turned_ref.shape[0]):
        turned_ref[index] = factor_ref[index * block:(index + 1) * block, :].T
    for index in range(slots // UNROLL):
        @pl.when(index < chunks)
        def _():
            for copy in copies(index):
                copy.wait()


def item_kernel(owner_total, groups, count_ref, place_ref, user_id_ref, item_id_ref, user_ref, turned_ref, rating_ref,
                weight_ref, *refs):
    panel_refs, refs = refs[:-5], refs[-5:]
    keep_ref, send_ref, tile_ref, item_ref, total = refs
    live = count_ref[0]
    item_mask = place_ref[1]
    slots, block = rating_ref.shape[0], rating_ref.shape[1]
    row = 0
    for panel_ref in panel_refs:
        item_ref[row:row + panel_ref.shape[0], :] = panel_ref[...]
        row += panel_ref.shape[0]
    total[...] = jnp.zeros_like(total)
    turns = (live + WIDE - 1) // WIDE

    def turn(index, carry):
        base = index * WIDE
        predicted = []
        for step in range(WIDE):
            user_row = pl.multiple_of(user_id_ref[0, base + step] * block, block)
            item_row = pl.multiple_of((item_id_ref[0, base + step] ^ item_mask) * block, block)
            predicted.append(lax.dot_general(
                user_ref[pl.ds(user_row, block), :], item_ref[pl.ds(item_row, block), :],
                (((1,), (1,)), ((), ())), preferred_element_type=jnp.float32))
        terms = []
        for step in range(WIDE):
            slot = base + step
            weighted = weight_ref[slot].astype(jnp.float32) * (
                predicted[step] - rating_ref[slot].astype(jnp.float32))
            weighted = jnp.where(slot < live, weighted, 0.0).astype(jnp.bfloat16)
            tile_ref[slot] = weighted
            terms.append(jnp.dot(turned_ref[user_id_ref[0, slot]], weighted, preferred_element_type=jnp.float32))
        for step in range(WIDE):
            total[item_id_ref[0, base + step]] += terms[step]
        return carry

    lax.fori_loop(0, turns, turn, 0)
    own_place = place_ref[0]
    owned = keep_ref.shape[0] * 2 // owner_total
    half = owner_total // 2
    per_block = block // owned
    for item in range(total.shape[0]):
        rows = total[item].T
        for part in range(per_block):
            place = own_place ^ place_of(item * per_block + part, groups)
            piece = rows[part * owned:(part + 1) * owned]
            row = pl.multiple_of((place % half) * owned, owned)

            @pl.when(place < half)
            def _():
                keep_ref[pl.ds(row, owned), :] = piece

            @pl.when(place >= half)
            def _():
                send_ref[pl.ds(row, owned), :] = piece


def user_kernel(count_ref, place_ref, user_id_ref, item_id_ref, item_ref, tile_ref, total_ref, token_ref):
    item_mask = place_ref[1]
    block = tile_ref.shape[1]
    turns = (count_ref[0] + WIDE - 1) // WIDE
    token_ref[...] = jnp.zeros_like(token_ref)
    total_ref[...] = jnp.zeros_like(total_ref)

    def turn(index, carry):
        base = index * WIDE
        terms = []
        for step in range(WIDE):
            item_row = pl.multiple_of((item_id_ref[0, base + step] ^ item_mask) * block, block)
            terms.append(jnp.dot(tile_ref[base + step], item_ref[pl.ds(item_row, block), :],
                                 preferred_element_type=jnp.float32))
        for step in range(WIDE):
            user_row = pl.multiple_of(user_id_ref[0, base + step] * block, block)
            total_ref[pl.ds(user_row, block), :] += terms[step]
        return carry

    lax.fori_loop(0, turns, turn, 0)


def sum_kernel(term_total, token_ref, *refs):
    terms, parts = refs[:term_total], refs[term_total:]
    rows = parts[0].shape[0]
    for index, part in enumerate(parts):
        here = pl.ds(index * rows, rows)
        value = terms[0][here, :]
        for term in terms[1:]:
            value = value + term[here, :].astype(jnp.float32)
        part[...] = value.astype(part.dtype)


def sum_parts(terms, ways, token, sent):
    rows, rank = terms[0].shape
    shapes = [jax.ShapeDtypeStruct((rows // ways, rank), kind) for kind in [jnp.float32] + [sent] * (ways - 1)]
    return pl.pallas_call(
        functools.partial(sum_kernel, len(terms)),
        out_shape=tuple(shapes),
        in_specs=[VMEM] * (1 + len(terms)),
        out_specs=(VMEM,) * ways,
        compiler_params=pltpu.CompilerParams(vmem_limit_bytes=8 << 20),
        name="sum_parts",
    )(token, *terms)


def body(user_factors, item_factors, block_user, block_item, counts, ratings, weights):
    rank = user_factors.shape[1]
    slots, block = ratings.shape[1], ratings.shape[2]
    user_rows = user_factors.shape[0]
    panel_rows = item_factors.shape[0]
    panel_total = lax.axis_size("items")
    device_total = lax.axis_size("users") * panel_total
    panel_index = lax.axis_index("items")
    me = lax.axis_index("users") * panel_total + panel_index
    groups = phases_of(device_total)
    item_rows = panel_rows * panel_total
    turns = slots // UNROLL

    def permute(array, mask):
        return lax.ppermute(array, AXES, [(index, index ^ mask) for index in range(device_total)])

    def options(limit, micros):
        return dict(
            compiler_params=pltpu.CompilerParams(vmem_limit_bytes=limit << 20),
            cost_estimate=pl.CostEstimate(flops=0, bytes_accessed=int(3e6 * micros), transcendentals=0),
        )

    panels = [item_factors] + [permute(item_factors, mask) for mask in range(1, panel_total)]
    places = jnp.stack([place_of(me, groups), panel_index * (panel_rows // block)]).astype(jnp.int32)
    held = jax.ShapeDtypeStruct((slots, block, block), jnp.bfloat16)
    sems = pltpu.SemaphoreType.DMA((turns,))
    factors, turned, held_ratings, held_weights = pl.pallas_call(
        stage_kernel,
        out_shape=(
            jax.ShapeDtypeStruct((user_rows, rank), jnp.bfloat16),
            jax.ShapeDtypeStruct((user_rows // block, rank, block), jnp.bfloat16),
            held,
            held,
        ),
        in_specs=[SMEM] + [HBM] * 3,
        out_specs=(VMEM,) * 4,
        scratch_shapes=[pltpu.SemaphoreType.DMA, sems, sems],
        name="stage",
        **options(41, 6),
    )(counts, user_factors, ratings, weights)

    half_shape = jax.ShapeDtypeStruct((item_rows // 2, rank), jnp.float32)
    keep, send, weighted, item_whole = pl.pallas_call(
        functools.partial(item_kernel, device_total, groups),
        out_shape=(half_shape, half_shape, held, jax.ShapeDtypeStruct((item_rows, rank), jnp.bfloat16)),
        in_specs=[SMEM] * 4 + [VMEM] * (4 + panel_total),
        out_specs=(VMEM,) * 4,
        scratch_shapes=[pltpu.VMEM((item_rows // block, rank, block), jnp.float32)],
        name="item_sums",
        **options(12, 8),
    )(counts, places, block_user, block_item, factors, turned, held_ratings, held_weights, *panels)

    terms = [keep, permute(send, 1)]
    user_sums, user_token = pl.pallas_call(
        user_kernel,
        out_shape=(jax.ShapeDtypeStruct((user_rows, rank), jnp.float32), jax.ShapeDtypeStruct((8, 128), jnp.float32)),
        in_specs=[SMEM] * 4 + [VMEM] * 2,
        out_specs=(VMEM, VMEM),
        name="user_sums",
        **options(8, 5),
    )(counts, places, block_user, block_item, item_whole, weighted)
    token = jnp.zeros((8, 128), jnp.float32)
    for group in groups[1:]:
        ways = 1 << len(group)
        parts = sum_parts(terms, ways, token, jnp.bfloat16 if group is groups[1] else jnp.float32)
        token = user_token
        kept, late = lax.optimization_barrier((parts[0], me))
        terms = [kept]
        for way in reversed(range(1, ways)):
            mask = sum(((way >> index) & 1) << bit for index, bit in enumerate(group))
            terms.append(permute(parts[way], mask))
    partial = functools.reduce(jnp.add, terms)
    user_grad = user_sums * grad_scale + decay_rate * factors.astype(jnp.float32)
    owned_rows = partial.shape[0]
    first_row = late * owned_rows
    chosen = lax.div(first_row, panel_rows) ^ lax.rem(late, panel_total)
    pieces = [lax.dynamic_slice_in_dim(panel, lax.rem(first_row, panel_rows), owned_rows, 0) for panel in panels]
    own_factors = pieces[0]
    for index in range(1, panel_total):
        own_factors = jnp.where(chosen == index, pieces[index], own_factors)
    item_grad = partial * grad_scale + decay_rate * own_factors.astype(jnp.float32)
    return (user_grad, item_grad)


def solution(mesh):
    in_specs = (
        P(AXES, None),
        P("items", None),
        P(AXES, None),
        P(AXES, None),
        P(AXES),
        P(AXES, None, None, None),
        P(AXES, None, None, None),
    )
    out_specs = (P(AXES, None), P(AXES, None))
    return jax.shard_map(body, mesh=mesh, in_specs=in_specs, out_specs=out_specs, check_vma=False)
```

profile of v0, /device:TPU:0, one launch (start us, length us, event | category | flops | bytes accessed | tf_op | source)
XLA Modules:
  0.0 36.1 jit_solution(12013299142213487319)
XLA Ops:
  0.6 0.5 %collective-permute-start = (bf16[256,256]{1,0:T(8,128)(2,1)}, bf16[256,256]{1,0:T(8,128)(2,1)S(1)}, u32[]{:S(2)}, u32[]{:S(2)}) collective-permute-start(bf16[256,256]{1,0:T(8,128)(2,1)} %refs_0_.1), channel_id=1, source_target_pairs={{0,1},{1,0},{2,3},{3,2},{4,5},{5,4},{6,7},{7,6},{8,9},{9,8},{10,11... | collective-permute-start | bytes 393224 | tf_op jit(solution)/shard_map/ppermute | solution.py:181
  1.1 2.6 %collective-permute-start.1 = (bf16[256,256]{1,0:T(8,128)(2,1)}, bf16[256,256]{1,0:T(8,128)(2,1)S(1)}, u32[]{:S(2)}, u32[]{:S(2)}) collective-permute-start(bf16[256,256]{1,0:T(8,128)(2,1)} %refs_0_.1), channel_id=1, source_target_pairs={{0,2},{1,3},{2,0},{3,1},{4,6},{5,7},{6,4},{7,5},{8,10},{9,11},{10,... | collective-permute-start | bytes 393224 | tf_op jit(solution)/shard_map/ppermute | solution.py:181
  3.7 0.1 collective-permute-start.2
  4.5 0.0 copy-start
  4.5 1.2 %copy-done = bf16[2048,256]{1,0:T(8,128)(2,1)S(1)} copy-done((bf16[2048,256]{1,0:T(8,128)(2,1)S(1)}, bf16[2048,256]{1,0:T(8,128)(2,1)}, u32[]{:S(2)}) %copy-start) | copy-done | bytes 1048600
  5.7 0.0 copy-start.1
  5.7 0.0 copy-start.2
  5.7 0.0 copy-start.3
  5.7 2.7 %stage.1 = (bf16[2048,256]{1,0:T(8,128)(2,1)S(1)}, bf16[16,256,128]{2,1,0:T(8,128)(2,1)S(1)}, bf16[128,128,128]{2,1,0:T(8,128)(2,1)S(1)}, bf16[128,128,128]{2,1,0:T(8,128)(2,1)S(1)}) custom-call(s32[1]{0:T(128)S(6)} %copy.9.count_ref, bf16[2048,256]{1,0:T(8,128)(2,1)S(1)} %copy-done, bf16[1,128,128,128]{3,2,1,0:T(8,128)(2,1)} %rating_ref.1, ...), custom_call_target="tpu_custom_call" | custom-call | bytes 18000000 | tf_op jit(solution)/shard_map/stage/pallas_call | solution.py:193
  8.4 0.1 pad_add_fusion.place_ref
  8.5 0.0 collective-permute-done.refs_1_
  8.5 0.0 collective-permute-done.1.refs_2_
  8.5 2.1 %collective-permute-done.2.refs_3_ = bf16[256,256]{1,0:T(8,128)(2,1)S(1)} collective-permute-done((bf16[256,256]{1,0:T(8,128)(2,1)}, bf16[256,256]{1,0:T(8,128)(2,1)S(1)}, u32[]{:S(2)}, u32[]{:S(2)}) %collective-permute-start.2) | collective-permute-done | bytes 131104 | tf_op jit(solution)/shard_map/ppermute | solution.py:181
  10.6 0.0 copy-done.1
  10.6 0.0 copy-done.2
  10.6 0.0 copy-done.3
  10.6 5.6 %item_sums.1 = (f32[512,256]{1,0:T(8,128)S(1)}, f32[512,256]{1,0:T(8,128)S(1)}, bf16[128,128,128]{2,1,0:T(8,128)(2,1)S(1)}, bf16[1024,256]{1,0:T(8,128)(2,1)S(1)}) custom-call(s32[1]{0:T(128)S(6)} %copy.9.count_ref, s32[2]{0:T(128)S(1)} %pad_add_fusion.place_ref, s32[1,128]{1,0:T(1,128)S(1)} %copy-done.2, s32[1,128]{1,0:T(1,128)S(1)} %copy-done.3, ...), custom_call_target="tpu_custom_call" | custom-call | bytes 24000000 | tf_op jit(solution)/shard_map/item_sums/pallas_call | solution.py:209
  16.2 0.1 collective-permute-start.3
  16.2 1.9 %collective-permute-done.3.refs_1_ = f32[512,256]{1,0:T(8,128)S(1)} collective-permute-done((f32[512,256]{1,0:T(8,128)S(1)}, f32[512,256]{1,0:T(8,128)S(1)}, u32[]{:S(2)}, u32[]{:S(2)}) %collective-permute-start.3) | collective-permute-done | bytes 524320 | tf_op jit(solution)/shard_map/ppermute | solution.py:181
  18.1 0.1 sum_parts.2
  18.2 3.8 %collective-permute-start.4 = (bf16[128,256]{1,0:T(8,128)(2,1)S(1)}, bf16[128,256]{1,0:T(8,128)(2,1)S(1)}, u32[]{:S(2)}, u32[]{:S(2)}) collective-permute-start(bf16[128,256]{1,0:T(8,128)(2,1)S(1)} %get-tuple-element.35), channel_id=1, source_target_pairs={{0,6},{1,7},{2,4},{3,5},{4,2},{5,3},{6,0},{7,1},{8,14},{9,15},{10,... | collective-permute-start | bytes 196616 | tf_op jit(solution)/shard_map/ppermute | solution.py:181
  22.0 0.5 %collective-permute-start.5 = (bf16[128,256]{1,0:T(8,128)(2,1)S(1)}, bf16[128,256]{1,0:T(8,128)(2,1)S(1)}, u32[]{:S(2)}, u32[]{:S(2)}) collective-permute-start(bf16[128,256]{1,0:T(8,128)(2,1)S(1)} %get-tuple-element.36), channel_id=1, source_target_pairs={{0,4},{1,5},{2,6},{3,7},{4,0},{5,1},{6,2},{7,3},{8,12},{9,13},{10,... | collective-permute-start | bytes 196616 | tf_op jit(solution)/shard_map/ppermute | solution.py:181
  22.6 0.1 collective-permute-start.6
  22.7 3.0 %user_sums.1 = (f32[2048,256]{1,0:T(8,128)S(1)}, f32[8,128]{1,0:T(8,128)S(1)}) custom-call(s32[1]{0:T(128)S(6)} %copy.9.count_ref, s32[2]{0:T(128)S(1)} %pad_add_fusion.place_ref, s32[1,128]{1,0:T(1,128)S(1)} %copy-done.2, s32[1,128]{1,0:T(1,128)S(1)} %copy-done.3, bf16[1024,256]{1,0:T(8,128)(2,1)S(1)} %get-tuple-element.27.item_ref, ...), custom_call_target="tpu_custom_call" | custom-call | bytes 15000000 | tf_op jit(solution)/shard_map/user_sums/pallas_call | solution.py:220
  25.7 0.0 collective-permute-done.4.refs_1_
  25.7 0.6 %collective-permute-done.5.refs_2_ = bf16[128,256]{1,0:T(8,128)(2,1)S(1)} collective-permute-done((bf16[128,256]{1,0:T(8,128)(2,1)S(1)}, bf16[128,256]{1,0:T(8,128)(2,1)S(1)}, u32[]{:S(2)}, u32[]{:S(2)}) %collective-permute-start.5) | collective-permute-done | bytes 65568 | tf_op jit(solution)/shard_map/ppermute | solution.py:181
  26.3 0.5 %collective-permute-done.6.refs_3_ = bf16[128,256]{1,0:T(8,128)(2,1)S(1)} collective-permute-done((bf16[128,256]{1,0:T(8,128)(2,1)S(1)}, bf16[128,256]{1,0:T(8,128)(2,1)S(1)}, u32[]{:S(2)}, u32[]{:S(2)}) %collective-permute-start.6) | collective-permute-done | bytes 65568 | tf_op jit(solution)/shard_map/ppermute | solution.py:181
  26.9 3.7 %collective-permute-start.7 = (f32[32,256]{1,0:T(8,128)S(1)}, f32[32,256]{1,0:T(8,128)S(1)}, u32[]{:S(2)}, u32[]{:S(2)}) collective-permute-start(f32[32,256]{1,0:T(8,128)S(1)} %get-tuple-element.40), channel_id=1, source_target_pairs={{0,24},{1,25},{2,26},{3,27},{4,28},{5,29},{6,30},{7,31},{8,16},{9,... | collective-permute-start | bytes 98312 | tf_op jit(solution)/shard_map/ppermute | solution.py:181
  30.6 0.0 collective-permute-start.8
  30.6 0.7 %collective-permute-start.9 = (f32[32,256]{1,0:T(8,128)S(1)}, f32[32,256]{1,0:T(8,128)S(1)}, u32[]{:S(2)}, u32[]{:S(2)}) collective-permute-start(f32[32,256]{1,0:T(8,128)S(1)} %get-tuple-element.42), channel_id=1, source_target_pairs={{0,8},{1,9},{2,10},{3,11},{4,12},{5,13},{6,14},{7,15},{8,0},{9,1},... | collective-permute-start | bytes 98312 | tf_op jit(solution)/shard_map/ppermute | solution.py:181
  31.3 1.7 %multiply_add_fusion = f32[2048,256]{1,0:T(8,128)} fusion(bf16[2048,256]{1,0:T(8,128)(2,1)S(1)} %get-tuple-element.23.user_ref, f32[2048,256]{1,0:T(8,128)S(1)} %get-tuple-element.29), kind=kLoop, calls=%fused_computation | loop fusion | flops 2097152 | bytes 5242880 | tf_op jit(solution)/shard_map/add | solution.py:239
  33.0 0.0 collective-permute-done.7
  33.1 2.4 %collective-permute-done.8 = f32[32,256]{1,0:T(8,128)S(1)} collective-permute-done((f32[32,256]{1,0:T(8,128)S(1)}, f32[32,256]{1,0:T(8,128)S(1)}, u32[]{:S(2)}, u32[]{:S(2)}) %collective-permute-start.8) | collective-permute-done | bytes 32800 | tf_op jit(solution)/shard_map/ppermute | solution.py:181
  35.4 0.0 collective-permute-done.9
  35.4 0.6 %multiply_add_fusion.1 = f32[32,256]{1,0:T(8,128)} fusion(f32[32,256]{1,0:T(8,128)S(1)} %collective-permute-done.9, f32[32,256]{1,0:T(8,128)S(1)} %collective-permute-done.8, f32[32,256]{1,0:T(8,128)S(1)} %get-tuple-element.39, f32[32,256]{1,0:T(8,128)S(1)} %collective-permute-done.7, bf16[256,256]{1,0:T(8,128)(2,1)S(1)} %copy-done.1, s32[]{:T(128)S(6)} %select_n.27, ...), kind=kLoop, calls=%fused_computation.1 | loop fusion | flops 81920 | bytes 229383 | tf_op jit(solution)/shard_map/add | solution.py:247
  (2 shorter events, 0.0 us)
Async XLA Ops:
  0.6 7.9 %collective-permute-start = (bf16[256,256]{1,0:T(8,128)(2,1)}, bf16[256,256]{1,0:T(8,128)(2,1)S(1)}, u32[]{:S(2)}, u32[]{:S(2)}) collective-permute-start(bf16[256,256]{1,0:T(8,128)(2,1)} %refs_0_.1), channel_id=1, source_target_pairs={{0,1},{1,0},{2,3},{3,2},{4,5},{5,4},{6,7},{7,6},{8,9},{9,8},{10,11... | collective-permute-start | bytes 393224 | tf_op jit(solution)/shard_map/ppermute | solution.py:181
  1.1 7.3 %collective-permute-start.1 = (bf16[256,256]{1,0:T(8,128)(2,1)}, bf16[256,256]{1,0:T(8,128)(2,1)S(1)}, u32[]{:S(2)}, u32[]{:S(2)}) collective-permute-start(bf16[256,256]{1,0:T(8,128)(2,1)} %refs_0_.1), channel_id=1, source_target_pairs={{0,2},{1,3},{2,0},{3,1},{4,6},{5,7},{6,4},{7,5},{8,10},{9,11},{10,... | collective-permute-start | bytes 393224 | tf_op jit(solution)/shard_map/ppermute | solution.py:181
  3.7 6.8 %collective-permute-start.2 = (bf16[256,256]{1,0:T(8,128)(2,1)}, bf16[256,256]{1,0:T(8,128)(2,1)S(1)}, u32[]{:S(2)}, u32[]{:S(2)}) collective-permute-start(bf16[256,256]{1,0:T(8,128)(2,1)} %refs_0_.1), channel_id=1, source_target_pairs={{0,3},{1,2},{2,1},{3,0},{4,7},{5,6},{6,5},{7,4},{8,11},{9,10},{10,... | collective-permute-start | bytes 393224 | tf_op jit(solution)/shard_map/ppermute | solution.py:181
  4.5 1.2 %copy-start = (bf16[2048,256]{1,0:T(8,128)(2,1)S(1)}, bf16[2048,256]{1,0:T(8,128)(2,1)}, u32[]{:S(2)}) copy-start(bf16[2048,256]{1,0:T(8,128)(2,1)} %user_ref.1) | copy-start | bytes 3145732
  5.7 4.9 %copy-start.1 = (bf16[256,256]{1,0:T(8,128)(2,1)S(1)}, bf16[256,256]{1,0:T(8,128)(2,1)}, u32[]{:S(2)}) copy-start(bf16[256,256]{1,0:T(8,128)(2,1)} %refs_0_.1) | copy-start | bytes 393220
  5.7 4.9 %copy-start.2 = (s32[1,128]{1,0:T(1,128)S(1)}, s32[1,128]{1,0:T(1,128)}, u32[]{:S(2)}) copy-start(s32[1,128]{1,0:T(1,128)} %user_id_ref.3) | copy-start | bytes 1540
  5.7 4.9 %copy-start.3 = (s32[1,128]{1,0:T(1,128)S(1)}, s32[1,128]{1,0:T(1,128)}, u32[]{:S(2)}) copy-start(s32[1,128]{1,0:T(1,128)} %item_id_ref.3) | copy-start | bytes 1540
  16.2 2.0 %collective-permute-start.3 = (f32[512,256]{1,0:T(8,128)S(1)}, f32[512,256]{1,0:T(8,128)S(1)}, u32[]{:S(2)}, u32[]{:S(2)}) collective-permute-start(f32[512,256]{1,0:T(8,128)S(1)} %get-tuple-element.32), channel_id=1, source_target_pairs={{0,1},{1,0},{2,3},{3,2},{4,5},{5,4},{6,7},{7,6},{8,9},{9,8},{10,11... | collective-permute-start | bytes 1572872 | tf_op jit(solution)/shard_map/ppermute | solution.py:181
  18.2 7.5 %collective-permute-start.4 = (bf16[128,256]{1,0:T(8,128)(2,1)S(1)}, bf16[128,256]{1,0:T(8,128)(2,1)S(1)}, u32[]{:S(2)}, u32[]{:S(2)}) collective-permute-start(bf16[128,256]{1,0:T(8,128)(2,1)S(1)} %get-tuple-element.35), channel_id=1, source_target_pairs={{0,6},{1,7},{2,4},{3,5},{4,2},{5,3},{6,0},{7,1},{8,14},{9,15},{10,... | collective-permute-start | bytes 196616 | tf_op jit(solution)/shard_map/ppermute | solution.py:181
  22.0 4.3 %collective-permute-start.5 = (bf16[128,256]{1,0:T(8,128)(2,1)S(1)}, bf16[128,256]{1,0:T(8,128)(2,1)S(1)}, u32[]{:S(2)}, u32[]{:S(2)}) collective-permute-start(bf16[128,256]{1,0:T(8,128)(2,1)S(1)} %get-tuple-element.36), channel_id=1, source_target_pairs={{0,4},{1,5},{2,6},{3,7},{4,0},{5,1},{6,2},{7,3},{8,12},{9,13},{10,... | collective-permute-start | bytes 196616 | tf_op jit(solution)/shard_map/ppermute | solution.py:181
  22.6 4.3 %collective-permute-start.6 = (bf16[128,256]{1,0:T(8,128)(2,1)S(1)}, bf16[128,256]{1,0:T(8,128)(2,1)S(1)}, u32[]{:S(2)}, u32[]{:S(2)}) collective-permute-start(bf16[128,256]{1,0:T(8,128)(2,1)S(1)} %get-tuple-element.37), channel_id=1, source_target_pairs={{0,2},{1,3},{2,0},{3,1},{4,6},{5,7},{6,4},{7,5},{8,10},{9,11},{10,... | collective-permute-start | bytes 196616 | tf_op jit(solution)/shard_map/ppermute | solution.py:181
  26.9 6.2 %collective-permute-start.7 = (f32[32,256]{1,0:T(8,128)S(1)}, f32[32,256]{1,0:T(8,128)S(1)}, u32[]{:S(2)}, u32[]{:S(2)}) collective-permute-start(f32[32,256]{1,0:T(8,128)S(1)} %get-tuple-element.40), channel_id=1, source_target_pairs={{0,24},{1,25},{2,26},{3,27},{4,28},{5,29},{6,30},{7,31},{8,16},{9,... | collective-permute-start | bytes 98312 | tf_op jit(solution)/shard_map/ppermute | solution.py:181
  30.6 4.8 %collective-permute-start.8 = (f32[32,256]{1,0:T(8,128)S(1)}, f32[32,256]{1,0:T(8,128)S(1)}, u32[]{:S(2)}, u32[]{:S(2)}) collective-permute-start(f32[32,256]{1,0:T(8,128)S(1)} %get-tuple-element.41), channel_id=1, source_target_pairs={{0,16},{1,17},{2,18},{3,19},{4,20},{5,21},{6,22},{7,23},{8,24},{9,... | collective-permute-start | bytes 98312 | tf_op jit(solution)/shard_map/ppermute | solution.py:181
  30.6 4.8 %collective-permute-start.9 = (f32[32,256]{1,0:T(8,128)S(1)}, f32[32,256]{1,0:T(8,128)S(1)}, u32[]{:S(2)}, u32[]{:S(2)}) collective-permute-start(f32[32,256]{1,0:T(8,128)S(1)} %get-tuple-element.42), channel_id=1, source_target_pairs={{0,8},{1,9},{2,10},{3,11},{4,12},{5,13},{6,14},{7,15},{8,0},{9,1},... | collective-permute-start | bytes 98312 | tf_op jit(solution)/shard_map/ppermute | solution.py:181
where the time goes:
time: 36.2 us; the launch traced here: 36.1 us
  starting transfers between devices  12.2 us (34%)
  Pallas kernels  11.4 us (31%)
  waiting for transfers between devices  7.53 us (21%)
  other arithmetic  2.42 us (7%)
  between operations  1.36 us (4%)
  local copies, waits for them, and re-layouts  1.23 us (3%)
    ppermute x10, starting transfers between devices, permute(): lax.ppermute(array, AXES, [(index, index ^ mask) for index in range(devic...  12.2 us
    ppermute x10, waiting for transfers between devices, permute(): lax.ppermute(array, AXES, [(index, index ^ mask) for index in range(devic...  7.53 us
    pallas_call x1, Pallas kernels, body(): pl.pallas_call(functools.partial(item_kernel, device_total, groups), out_...  5.56 us
    pallas_call x1, Pallas kernels, body(): pl.pallas_call(user_kernel, out_shape=(jax.ShapeDtypeStruct((user_rows, r...  3.02 us
    pallas_call x1, Pallas kernels, body(): pl.pallas_call(stage_kernel, out_shape=(jax.ShapeDtypeStruct((user_rows,...  2.7 us
    add x1, other arithmetic, body(): user_sums * grad_scale + decay_rate * factors.astype(jnp.float32)  1.7 us
    unnamed x8, local copies, waits for them, and re-layouts  1.23 us
  transfers between devices with their start and end apart: 10, of which 5 were waited for; matrix products, arithmetic and copies ran while one was open for 5% of the time, Pallas kernels for 16%

commit v1 on v0

--- a/solution.py
+++ b/solution.py
@@ -33,9 +33,9 @@
     return place
 
 
-def stage_kernel(count_ref, user_ref, rating_ref, weight_ref, factor_ref, turned_ref, held_rating_ref, held_weight_ref,
-                 factor_sem, rating_sems, weight_sems):
-    slots, block = held_rating_ref.shape[0], held_rating_ref.shape[1]
+def stage_kernel(count_ref, place_ref, rating_ref, weight_ref, held_rating_ref, held_weight_ref, token_ref, rating_sems,
+                 weight_sems):
+    slots = held_rating_ref.shape[0]
     chunks = (count_ref[0] + UNROLL - 1) // UNROLL
 
     def copies(index):
@@ -45,16 +45,12 @@
             pltpu.make_async_copy(weight_ref.at[0, part], held_weight_ref.at[part], weight_sems.at[index]),
         )
 
-    factor_copy = pltpu.make_async_copy(user_ref, factor_ref, factor_sem)
-    factor_copy.start()
     for index in range(slots // UNROLL):
         @pl.when(index < chunks)
         def _():
             for copy in copies(index):
                 copy.start()
-    factor_copy.wait()
-    for index in range(turned_ref.shape[0]):
-        turned_ref[index] = factor_ref[index * block:(index + 1) * block, :].T
+    token_ref[...] = jnp.zeros_like(token_ref) + place_ref[0].astype(jnp.float32)
     for index in range(slots // UNROLL):
         @pl.when(index < chunks)
         def _():
@@ -62,7 +58,7 @@
                 copy.wait()
 
 
-def item_kernel(owner_total, groups, count_ref, place_ref, user_id_ref, item_id_ref, user_ref, turned_ref, rating_ref,
+def item_kernel(owner_total, groups, count_ref, place_ref, user_id_ref, item_id_ref, user_ref, token_ref, rating_ref,
                 weight_ref, *refs):
     panel_refs, refs = refs[:-5], refs[-5:]
     keep_ref, send_ref, tile_ref, item_ref, total = refs
@@ -92,7 +88,10 @@
                 predicted[step] - rating_ref[slot].astype(jnp.float32))
             weighted = jnp.where(slot < live, weighted, 0.0).astype(jnp.bfloat16)
             tile_ref[slot] = weighted
-            terms.append(jnp.dot(turned_ref[user_id_ref[0, slot]], weighted, preferred_element_type=jnp.float32))
+            user_row = pl.multiple_of(user_id_ref[0, slot] * block, block)
+            terms.append(lax.dot_general(
+                weighted, user_ref[pl.ds(user_row, block), :],
+                (((0,), (0,)), ((), ())), preferred_element_type=jnp.float32))
         for step in range(WIDE):
             total[item_id_ref[0, base + step]] += terms[step]
         return carry
@@ -102,20 +101,15 @@
     owned = keep_ref.shape[0] * 2 // owner_total
     half = owner_total // 2
     per_block = block // owned
-    for item in range(total.shape[0]):
-        rows = total[item].T
-        for part in range(per_block):
-            place = own_place ^ place_of(item * per_block + part, groups)
-            piece = rows[part * owned:(part + 1) * owned]
-            row = pl.multiple_of((place % half) * owned, owned)
-
-            @pl.when(place < half)
-            def _():
-                keep_ref[pl.ds(row, owned), :] = piece
-
-            @pl.when(place >= half)
-            def _():
-                send_ref[pl.ds(row, owned), :] = piece
+    for flip in range(2):
+        @pl.when(own_place // half == flip)
+        def _():
+            for owner in range(owner_total):
+                place = place_of(owner, groups)
+                target = send_ref if (place // half) ^ flip else keep_ref
+                row = pl.multiple_of(((own_place ^ place) % half) * owned, owned)
+                part = owner % per_block * owned
+                target[pl.ds(row, owned), :] = total[owner // per_block, part:part + owned, :]
 
 
 def user_kernel(count_ref, place_ref, user_id_ref, item_id_ref, item_ref, tile_ref, total_ref, token_ref):
@@ -186,24 +180,24 @@
             cost_estimate=pl.CostEstimate(flops=0, bytes_accessed=int(3e6 * micros), transcendentals=0),
         )
 
-    panels = [item_factors] + [permute(item_factors, mask) for mask in range(1, panel_total)]
     places = jnp.stack([place_of(me, groups), panel_index * (panel_rows // block)]).astype(jnp.int32)
     held = jax.ShapeDtypeStruct((slots, block, block), jnp.bfloat16)
     sems = pltpu.SemaphoreType.DMA((turns,))
-    factors, turned, held_ratings, held_weights = pl.pallas_call(
+    direct = {mask: permute(item_factors, mask) for mask in [*range(2, panel_total, 2), 1]}
+    held_ratings, held_weights, token = pl.pallas_call(
         stage_kernel,
-        out_shape=(
-            jax.ShapeDtypeStruct((user_rows, rank), jnp.bfloat16),
-            jax.ShapeDtypeStruct((user_rows // block, rank, block), jnp.bfloat16),
-            held,
-            held,
-        ),
-        in_specs=[SMEM] + [HBM] * 3,
-        out_specs=(VMEM,) * 4,
-        scratch_shapes=[pltpu.SemaphoreType.DMA, sems, sems],
+        out_shape=(held, held, jax.ShapeDtypeStruct((8, 128), jnp.float32)),
+        in_specs=[SMEM] * 2 + [HBM] * 2,
+        out_specs=(VMEM,) * 3,
+        scratch_shapes=[sems, sems],
         name="stage",
-        **options(41, 6),
-    )(counts, user_factors, ratings, weights)
+        **options(44, 6),
+    )(counts, places, ratings, weights)
+    panels = {0: item_factors, 1: direct[1]}
+    for mask in range(2, panel_total, 2):
+        panels[mask], token = lax.optimization_barrier((direct[mask], token))
+        panels[mask + 1] = permute(panels[mask], 1)
+    panels = [panels[mask] for mask in range(panel_total)]
 
     half_shape = jax.ShapeDtypeStruct((item_rows // 2, rank), jnp.float32)
     keep, send, weighted, item_whole = pl.pallas_call(
@@ -211,10 +205,10 @@
         out_shape=(half_shape, half_shape, held, jax.ShapeDtypeStruct((item_rows, rank), jnp.bfloat16)),
         in_specs=[SMEM] * 4 + [VMEM] * (4 + panel_total),
         out_specs=(VMEM,) * 4,
-        scratch_shapes=[pltpu.VMEM((item_rows // block, rank, block), jnp.float32)],
+        scratch_shapes=[pltpu.VMEM((item_rows // block, block, rank), jnp.float32)],
         name="item_sums",
         **options(12, 8),
-    )(counts, places, block_user, block_item, factors, turned, held_ratings, held_weights, *panels)
+    )(counts, places, block_user, block_item, user_factors, token, held_ratings, held_weights, *panels)
 
     terms = [keep, permute(send, 1)]
     user_sums, user_token = pl.pallas_call(
@@ -236,7 +230,7 @@
             mask = sum(((way >> index) & 1) << bit for index, bit in enumerate(group))
             terms.append(permute(parts[way], mask))
     partial = functools.reduce(jnp.add, terms)
-    user_grad = user_sums * grad_scale + decay_rate * factors.astype(jnp.float32)
+    user_grad = user_sums * grad_scale + decay_rate * user_factors.astype(jnp.float32)
     owned_rows = partial.shape[0]
     first_row = late * owned_rows
     chosen = lax.div(first_row, panel_rows) ^ lax.rem(late, panel_total)

time: 36.2 us -> 34 us (0.939)
  Pallas kernels: 11.4 us -> 5.58 us
  starting transfers between devices: 12.2 us -> 17.3 us
  local copies, waits for them, and re-layouts: 1.23 us -> 0.02 us
    ppermute x10, starting transfers between devices: 12.2 us -> 17.3 us  [permute(): lax.ppermute(array, AXES, [(index, index ^ mask) for index in range(devic...]
    pallas_call x1, Pallas kernels: 5.56 us -> 2.17 us  [body(): pl.pallas_call(functools.partial(item_kernel, device_total, groups), out_...]
    pallas_call x1, Pallas kernels: 3.02 us -> 1.44 us  [body(): pl.pallas_call(user_kernel, out_shape=(jax.ShapeDtypeStruct((user_rows, r...]
    unnamed x8, local copies, waits for them, and re-layouts: 1.23 us -> 0.01 us
    pallas_call x1, Pallas kernels: 2.7 us -> 1.89 us  [body(): pl.pallas_call(stage_kernel, out_shape=(held, held, jax.ShapeDtypeStruct(...]
  transfers between devices with their start and end apart: 10 -> 10, of which waited for: 5 -> 6; matrix products, arithmetic and copies ran while one was open for 5% -> 5% of each run, Pallas kernels for 16% -> 10%
where the time goes in v1:
time: 34 us; the launch traced here: 33.8 us
  starting transfers between devices  17.3 us (51%)
  waiting for transfers between devices  7.23 us (21%)
  Pallas kernels  5.58 us (16%)
  other arithmetic  2.3 us (7%)
  between operations  1.33 us (4%)
    ppermute x10, starting transfers between devices, permute(): lax.ppermute(array, AXES, [(index, index ^ mask) for index in range(devic...  17.3 us
    ppermute x10, waiting for transfers between devices, permute(): lax.ppermute(array, AXES, [(index, index ^ mask) for index in range(devic...  7.23 us
    pallas_call x1, Pallas kernels, body(): pl.pallas_call(functools.partial(item_kernel, device_total, groups), out_...  2.17 us
    pallas_call x1, Pallas kernels, body(): pl.pallas_call(stage_kernel, out_shape=(held, held, jax.ShapeDtypeStruct(...  1.89 us
    add x1, other arithmetic, body(): user_sums * grad_scale + decay_rate * user_factors.astype(jnp.float32)  1.59 us
    pallas_call x1, Pallas kernels, body(): pl.pallas_call(user_kernel, out_shape=(jax.ShapeDtypeStruct((user_rows, r...  1.44 us
  transfers between devices with their start and end apart: 10, of which 6 were waited for; matrix products, arithmetic and copies ran while one was open for 5% of the time, Pallas kernels for 10%

profile of v1, /device:TPU:0, one launch (start us, length us, event | category | flops | bytes accessed | tf_op | source)
XLA Modules:
  0.0 33.8 jit_solution(14192752313578852022)
XLA Ops:
  0.6 3.0 %collective-permute-start = (bf16[256,256]{1,0:T(8,128)(2,1)}, bf16[256,256]{1,0:T(8,128)(2,1)S(1)}, u32[]{:S(2)}, u32[]{:S(2)}) collective-permute-start(bf16[256,256]{1,0:T(8,128)(2,1)} %refs_0_.1), channel_id=1, source_target_pairs={{0,2},{1,3},{2,0},{3,1},{4,6},{5,7},{6,4},{7,5},{8,10},{9,11},{10,... | collective-permute-start | bytes 393224 | tf_op jit(solution)/shard_map/ppermute | solution.py:175
  3.7 0.0 collective-permute-start.1
  4.3 0.1 pad_add_fusion.place_ref
  4.4 0.0 copy-start
  4.4 0.0 copy-start.1
  4.4 0.0 copy-start.2
  4.4 0.0 copy-start.3
  4.4 1.9 %stage.1 = (bf16[128,128,128]{2,1,0:T(8,128)(2,1)S(1)}, bf16[128,128,128]{2,1,0:T(8,128)(2,1)S(1)}, f32[8,128]{1,0:T(8,128)S(1)}) custom-call(s32[1]{0:T(128)S(6)} %copy.9.count_ref, s32[2]{0:T(128)S(1)} %pad_add_fusion.place_ref, bf16[1,128,128,128]{3,2,1,0:T(8,128)(2,1)} %rating_ref.1, bf16[1,128,128,128]{3,2,1,0:T(8,128)(2,1)} %weight_ref.1), custom_call_target="tpu_custom_call" | custom-call | bytes 18000000 | tf_op jit(solution)/shard_map/stage/pallas_call | solution.py:187
  6.3 1.1 %collective-permute-done.refs_2_ = bf16[256,256]{1,0:T(8,128)(2,1)S(1)} collective-permute-done((bf16[256,256]{1,0:T(8,128)(2,1)}, bf16[256,256]{1,0:T(8,128)(2,1)S(1)}, u32[]{:S(2)}, u32[]{:S(2)}) %collective-permute-start) | collective-permute-done | bytes 131104 | tf_op jit(solution)/shard_map/ppermute | solution.py:175
  7.4 1.7 %collective-permute-start.2 = (bf16[256,256]{1,0:T(8,128)(2,1)S(1)}, bf16[256,256]{1,0:T(8,128)(2,1)S(1)}, u32[]{:S(2)}, u32[]{:S(2)}) collective-permute-start(bf16[256,256]{1,0:T(8,128)(2,1)S(1)} %collective-permute-done.refs_2_), channel_id=1, source_target_pairs={{0,1},{1,0},{2,3},{3,2},{4,5},{5,4},{6,7},{7,6},{8,9},{9,8},{10,11... | collective-permute-start | bytes 393224 | tf_op jit(solution)/shard_map/ppermute | solution.py:175
  9.1 0.0 collective-permute-done.1.refs_1_
  9.1 1.0 %collective-permute-done.2.refs_3_ = bf16[256,256]{1,0:T(8,128)(2,1)S(1)} collective-permute-done((bf16[256,256]{1,0:T(8,128)(2,1)S(1)}, bf16[256,256]{1,0:T(8,128)(2,1)S(1)}, u32[]{:S(2)}, u32[]{:S(2)}) %collective-permute-start.2) | collective-permute-done | bytes 131104 | tf_op jit(solution)/shard_map/ppermute | solution.py:175
  10.0 0.0 copy-done
  10.0 0.0 copy-done.1
  10.1 0.0 copy-done.2
  10.1 0.0 copy-done.3
  10.1 2.2 %item_sums.1 = (f32[512,256]{1,0:T(8,128)S(1)}, f32[512,256]{1,0:T(8,128)S(1)}, bf16[128,128,128]{2,1,0:T(8,128)(2,1)S(1)}, bf16[1024,256]{1,0:T(8,128)(2,1)S(1)}) custom-call(s32[1]{0:T(128)S(6)} %copy.9.count_ref, s32[2]{0:T(128)S(1)} %pad_add_fusion.place_ref, s32[1,128]{1,0:T(1,128)S(1)} %copy-done.2, s32[1,128]{1,0:T(1,128)S(1)} %copy-done.3, ...), custom_call_target="tpu_custom_call" | custom-call | bytes 24000000 | tf_op jit(solution)/shard_map/item_sums/pallas_call | solution.py:203
  12.2 4.5 %collective-permute-start.3 = (f32[512,256]{1,0:T(8,128)S(1)}, f32[512,256]{1,0:T(8,128)S(1)}, u32[]{:S(2)}, u32[]{:S(2)}) collective-permute-start(f32[512,256]{1,0:T(8,128)S(1)} %get-tuple-element.34), channel_id=1, source_target_pairs={{0,1},{1,0},{2,3},{3,2},{4,5},{5,4},{6,7},{7,6},{8,9},{9,8},{10,11... | collective-permute-start | bytes 1572872 | tf_op jit(solution)/shard_map/ppermute | solution.py:175
  16.8 1.5 %collective-permute-done.3.refs_1_ = f32[512,256]{1,0:T(8,128)S(1)} collective-permute-done((f32[512,256]{1,0:T(8,128)S(1)}, f32[512,256]{1,0:T(8,128)S(1)}, u32[]{:S(2)}, u32[]{:S(2)}) %collective-permute-start.3) | collective-permute-done | bytes 524320 | tf_op jit(solution)/shard_map/ppermute | solution.py:175
  18.3 0.1 sum_parts.2
  18.4 1.2 %collective-permute-start.4 = (bf16[128,256]{1,0:T(8,128)(2,1)S(1)}, bf16[128,256]{1,0:T(8,128)(2,1)S(1)}, u32[]{:S(2)}, u32[]{:S(2)}) collective-permute-start(bf16[128,256]{1,0:T(8,128)(2,1)S(1)} %get-tuple-element.37), channel_id=1, source_target_pairs={{0,6},{1,7},{2,4},{3,5},{4,2},{5,3},{6,0},{7,1},{8,14},{9,15},{10,... | collective-permute-start | bytes 196616 | tf_op jit(solution)/shard_map/ppermute | solution.py:175
  19.6 0.3 collective-permute-start.5
  19.9 2.1 %collective-permute-start.6 = (bf16[128,256]{1,0:T(8,128)(2,1)S(1)}, bf16[128,256]{1,0:T(8,128)(2,1)S(1)}, u32[]{:S(2)}, u32[]{:S(2)}) collective-permute-start(bf16[128,256]{1,0:T(8,128)(2,1)S(1)} %get-tuple-element.39), channel_id=1, source_target_pairs={{0,2},{1,3},{2,0},{3,1},{4,6},{5,7},{6,4},{7,5},{8,10},{9,11},{10,... | collective-permute-start | bytes 196616 | tf_op jit(solution)/shard_map/ppermute | solution.py:175
  21.9 1.4 %user_sums.1 = (f32[2048,256]{1,0:T(8,128)S(1)}, f32[8,128]{1,0:T(8,128)S(1)}) custom-call(s32[1]{0:T(128)S(6)} %copy.9.count_ref, s32[2]{0:T(128)S(1)} %pad_add_fusion.place_ref, s32[1,128]{1,0:T(1,128)S(1)} %copy-done.2, s32[1,128]{1,0:T(1,128)S(1)} %copy-done.3, bf16[1024,256]{1,0:T(8,128)(2,1)S(1)} %get-tuple-element.29.item_ref, ...), custom_call_target="tpu_custom_call" | custom-call | bytes 15000000 | tf_op jit(solution)/shard_map/user_sums/pallas_call | solution.py:214
  23.4 0.9 %collective-permute-done.4.refs_1_ = bf16[128,256]{1,0:T(8,128)(2,1)S(1)} collective-permute-done((bf16[128,256]{1,0:T(8,128)(2,1)S(1)}, bf16[128,256]{1,0:T(8,128)(2,1)S(1)}, u32[]{:S(2)}, u32[]{:S(2)}) %collective-permute-start.4) | collective-permute-done | bytes 65568 | tf_op jit(solution)/shard_map/ppermute | solution.py:175
  24.3 0.0 collective-permute-done.5.refs_2_
  24.3 0.8 %collective-permute-done.6.refs_3_ = bf16[128,256]{1,0:T(8,128)(2,1)S(1)} collective-permute-done((bf16[128,256]{1,0:T(8,128)(2,1)S(1)}, bf16[128,256]{1,0:T(8,128)(2,1)S(1)}, u32[]{:S(2)}, u32[]{:S(2)}) %collective-permute-start.6) | collective-permute-done | bytes 65568 | tf_op jit(solution)/shard_map/ppermute | solution.py:175
  25.1 3.1 %collective-permute-start.7 = (f32[32,256]{1,0:T(8,128)S(1)}, f32[32,256]{1,0:T(8,128)S(1)}, u32[]{:S(2)}, u32[]{:S(2)}) collective-permute-start(f32[32,256]{1,0:T(8,128)S(1)} %get-tuple-element.42), channel_id=1, source_target_pairs={{0,24},{1,25},{2,26},{3,27},{4,28},{5,29},{6,30},{7,31},{8,16},{9,... | collective-permute-start | bytes 98312 | tf_op jit(solution)/shard_map/ppermute | solution.py:175
  28.3 0.0 collective-permute-start.8
  28.3 1.3 %collective-permute-start.9 = (f32[32,256]{1,0:T(8,128)S(1)}, f32[32,256]{1,0:T(8,128)S(1)}, u32[]{:S(2)}, u32[]{:S(2)}) collective-permute-start(f32[32,256]{1,0:T(8,128)S(1)} %get-tuple-element.44), channel_id=1, source_target_pairs={{0,8},{1,9},{2,10},{3,11},{4,12},{5,13},{6,14},{7,15},{8,0},{9,1},... | collective-permute-start | bytes 98312 | tf_op jit(solution)/shard_map/ppermute | solution.py:175
  29.6 1.6 %multiply_add_fusion = f32[2048,256]{1,0:T(8,128)} fusion(bf16[2048,256]{1,0:T(8,128)(2,1)S(1)} %copy-done, f32[2048,256]{1,0:T(8,128)S(1)} %get-tuple-element.31), kind=kLoop, calls=%fused_computation | loop fusion | flops 2097152 | bytes 5242880 | tf_op jit(solution)/shard_map/add | solution.py:233
  31.2 0.0 collective-permute-done.7
  31.2 1.9 %collective-permute-done.8 = f32[32,256]{1,0:T(8,128)S(1)} collective-permute-done((f32[32,256]{1,0:T(8,128)S(1)}, f32[32,256]{1,0:T(8,128)S(1)}, u32[]{:S(2)}, u32[]{:S(2)}) %collective-permute-start.8) | collective-permute-done | bytes 32800 | tf_op jit(solution)/shard_map/ppermute | solution.py:175
  33.1 0.0 collective-permute-done.9
  33.1 0.6 %multiply_add_fusion.1 = f32[32,256]{1,0:T(8,128)} fusion(f32[32,256]{1,0:T(8,128)S(1)} %collective-permute-done.9, f32[32,256]{1,0:T(8,128)S(1)} %collective-permute-done.8, f32[32,256]{1,0:T(8,128)S(1)} %get-tuple-element.41, f32[32,256]{1,0:T(8,128)S(1)} %collective-permute-done.7, bf16[256,256]{1,0:T(8,128)(2,1)S(1)} %copy-done.1, s32[]{:T(128)S(6)} %select_n.27, ...), kind=kLoop, calls=%fused_computation.1 | loop fusion | flops 81920 | bytes 229383 | tf_op jit(solution)/shard_map/add | solution.py:241
  (2 shorter events, 0.0 us)
Async XLA Ops:
  0.6 6.7 %collective-permute-start = (bf16[256,256]{1,0:T(8,128)(2,1)}, bf16[256,256]{1,0:T(8,128)(2,1)S(1)}, u32[]{:S(2)}, u32[]{:S(2)}) collective-permute-start(bf16[256,256]{1,0:T(8,128)(2,1)} %refs_0_.1), channel_id=1, source_target_pairs={{0,2},{1,3},{2,0},{3,1},{4,6},{5,7},{6,4},{7,5},{8,10},{9,11},{10,... | collective-permute-start | bytes 393224 | tf_op jit(solution)/shard_map/ppermute | solution.py:175
  3.7 5.4 %collective-permute-start.1 = (bf16[256,256]{1,0:T(8,128)(2,1)}, bf16[256,256]{1,0:T(8,128)(2,1)S(1)}, u32[]{:S(2)}, u32[]{:S(2)}) collective-permute-start(bf16[256,256]{1,0:T(8,128)(2,1)} %refs_0_.1), channel_id=1, source_target_pairs={{0,1},{1,0},{2,3},{3,2},{4,5},{5,4},{6,7},{7,6},{8,9},{9,8},{10,11... | collective-permute-start | bytes 393224 | tf_op jit(solution)/shard_map/ppermute | solution.py:175
  4.4 5.7 %copy-start = (bf16[2048,256]{1,0:T(8,128)(2,1)S(1)}, bf16[2048,256]{1,0:T(8,128)(2,1)}, u32[]{:S(2)}) copy-start(bf16[2048,256]{1,0:T(8,128)(2,1)} %user_ref.1) | copy-start | bytes 3145732
  4.4 5.7 %copy-start.1 = (bf16[256,256]{1,0:T(8,128)(2,1)S(1)}, bf16[256,256]{1,0:T(8,128)(2,1)}, u32[]{:S(2)}) copy-start(bf16[256,256]{1,0:T(8,128)(2,1)} %refs_0_.1) | copy-start | bytes 393220
  4.4 5.7 %copy-start.2 = (s32[1,128]{1,0:T(1,128)S(1)}, s32[1,128]{1,0:T(1,128)}, u32[]{:S(2)}) copy-start(s32[1,128]{1,0:T(1,128)} %user_id_ref.3) | copy-start | bytes 1540
  4.4 5.7 %copy-start.3 = (s32[1,128]{1,0:T(1,128)S(1)}, s32[1,128]{1,0:T(1,128)}, u32[]{:S(2)}) copy-start(s32[1,128]{1,0:T(1,128)} %item_id_ref.3) | copy-start | bytes 1540
  7.4 2.7 %collective-permute-start.2 = (bf16[256,256]{1,0:T(8,128)(2,1)S(1)}, bf16[256,256]{1,0:T(8,128)(2,1)S(1)}, u32[]{:S(2)}, u32[]{:S(2)}) collective-permute-start(bf16[256,256]{1,0:T(8,128)(2,1)S(1)} %collective-permute-done.refs_2_), channel_id=1, source_target_pairs={{0,1},{1,0},{2,3},{3,2},{4,5},{5,4},{6,7},{7,6},{8,9},{9,8},{10,11... | collective-permute-start | bytes 393224 | tf_op jit(solution)/shard_map/ppermute | solution.py:175
  12.2 6.1 %collective-permute-start.3 = (f32[512,256]{1,0:T(8,128)S(1)}, f32[512,256]{1,0:T(8,128)S(1)}, u32[]{:S(2)}, u32[]{:S(2)}) collective-permute-start(f32[512,256]{1,0:T(8,128)S(1)} %get-tuple-element.34), channel_id=1, source_target_pairs={{0,1},{1,0},{2,3},{3,2},{4,5},{5,4},{6,7},{7,6},{8,9},{9,8},{10,11... | collective-permute-start | bytes 1572872 | tf_op jit(solution)/shard_map/ppermute | solution.py:175
  18.4 5.9 %collective-permute-start.4 = (bf16[128,256]{1,0:T(8,128)(2,1)S(1)}, bf16[128,256]{1,0:T(8,128)(2,1)S(1)}, u32[]{:S(2)}, u32[]{:S(2)}) collective-permute-start(bf16[128,256]{1,0:T(8,128)(2,1)S(1)} %get-tuple-element.37), channel_id=1, source_target_pairs={{0,6},{1,7},{2,4},{3,5},{4,2},{5,3},{6,0},{7,1},{8,14},{9,15},{10,... | collective-permute-start | bytes 196616 | tf_op jit(solution)/shard_map/ppermute | solution.py:175
  19.6 4.7 %collective-permute-start.5 = (bf16[128,256]{1,0:T(8,128)(2,1)S(1)}, bf16[128,256]{1,0:T(8,128)(2,1)S(1)}, u32[]{:S(2)}, u32[]{:S(2)}) collective-permute-start(bf16[128,256]{1,0:T(8,128)(2,1)S(1)} %get-tuple-element.38), channel_id=1, source_target_pairs={{0,4},{1,5},{2,6},{3,7},{4,0},{5,1},{6,2},{7,3},{8,12},{9,13},{10,... | collective-permute-start | bytes 196616 | tf_op jit(solution)/shard_map/ppermute | solution.py:175
  19.9 5.2 %collective-permute-start.6 = (bf16[128,256]{1,0:T(8,128)(2,1)S(1)}, bf16[128,256]{1,0:T(8,128)(2,1)S(1)}, u32[]{:S(2)}, u32[]{:S(2)}) collective-permute-start(bf16[128,256]{1,0:T(8,128)(2,1)S(1)} %get-tuple-element.39), channel_id=1, source_target_pairs={{0,2},{1,3},{2,0},{3,1},{4,6},{5,7},{6,4},{7,5},{8,10},{9,11},{10,... | collective-permute-start | bytes 196616 | tf_op jit(solution)/shard_map/ppermute | solution.py:175
  25.1 6.0 %collective-permute-start.7 = (f32[32,256]{1,0:T(8,128)S(1)}, f32[32,256]{1,0:T(8,128)S(1)}, u32[]{:S(2)}, u32[]{:S(2)}) collective-permute-start(f32[32,256]{1,0:T(8,128)S(1)} %get-tuple-element.42), channel_id=1, source_target_pairs={{0,24},{1,25},{2,26},{3,27},{4,28},{5,29},{6,30},{7,31},{8,16},{9,... | collective-permute-start | bytes 98312 | tf_op jit(solution)/shard_map/ppermute | solution.py:175
  28.3 4.8 %collective-permute-start.8 = (f32[32,256]{1,0:T(8,128)S(1)}, f32[32,256]{1,0:T(8,128)S(1)}, u32[]{:S(2)}, u32[]{:S(2)}) collective-permute-start(f32[32,256]{1,0:T(8,128)S(1)} %get-tuple-element.43), channel_id=1, source_target_pairs={{0,16},{1,17},{2,18},{3,19},{4,20},{5,21},{6,22},{7,23},{8,24},{9,... | collective-permute-start | bytes 98312 | tf_op jit(solution)/shard_map/ppermute | solution.py:175
  28.3 4.8 %collective-permute-start.9 = (f32[32,256]{1,0:T(8,128)S(1)}, f32[32,256]{1,0:T(8,128)S(1)}, u32[]{:S(2)}, u32[]{:S(2)}) collective-permute-start(f32[32,256]{1,0:T(8,128)S(1)} %get-tuple-element.44), channel_id=1, source_target_pairs={{0,8},{1,9},{2,10},{3,11},{4,12},{5,13},{6,14},{7,15},{8,0},{9,1},... | collective-permute-start | bytes 98312 | tf_op jit(solution)/shard_map/ppermute | solution.py:175

commit v2 on v1

--- a/solution.py
+++ b/solution.py
@@ -12,6 +12,7 @@
 AXES = ("users", "items")
 UNROLL = 16
 WIDE = 32
+WIDEST = 64
 VMEM = pl.BlockSpec(memory_space=pltpu.VMEM)
 SMEM = pl.BlockSpec(memory_space=pltpu.SMEM)
 HBM = pl.BlockSpec(memory_space=pltpu.HBM)
@@ -70,19 +71,19 @@
         item_ref[row:row + panel_ref.shape[0], :] = panel_ref[...]
         row += panel_ref.shape[0]
     total[...] = jnp.zeros_like(total)
-    turns = (live + WIDE - 1) // WIDE
+    turns = (live + WIDEST - 1) // WIDEST
 
     def turn(index, carry):
-        base = index * WIDE
+        base = index * WIDEST
         predicted = []
-        for step in range(WIDE):
+        for step in range(WIDEST):
             user_row = pl.multiple_of(user_id_ref[0, base + step] * block, block)
             item_row = pl.multiple_of((item_id_ref[0, base + step] ^ item_mask) * block, block)
             predicted.append(lax.dot_general(
                 user_ref[pl.ds(user_row, block), :], item_ref[pl.ds(item_row, block), :],
                 (((1,), (1,)), ((), ())), preferred_element_type=jnp.float32))
         terms = []
-        for step in range(WIDE):
+        for step in range(WIDEST):
             slot = base + step
             weighted = weight_ref[slot].astype(jnp.float32) * (
                 predicted[step] - rating_ref[slot].astype(jnp.float32))
@@ -92,7 +93,7 @@
             terms.append(lax.dot_general(
                 weighted, user_ref[pl.ds(user_row, block), :],
                 (((0,), (0,)), ((), ())), preferred_element_type=jnp.float32))
-        for step in range(WIDE):
+        for step in range(WIDEST):
             total[item_id_ref[0, base + step]] += terms[step]
         return carry
 
@@ -109,7 +110,8 @@
                 target = send_ref if (place // half) ^ flip else keep_ref
                 row = pl.multiple_of(((own_place ^ place) % half) * owned, owned)
                 part = owner % per_block * owned
-                target[pl.ds(row, owned), :] = total[owner // per_block, part:part + owned, :]
+                piece = total[owner // per_block, part:part + owned, :]
+                target[pl.ds(row, owned), :] = piece.astype(target.dtype)
 
 
 def user_kernel(count_ref, place_ref, user_id_ref, item_id_ref, item_ref, tile_ref, total_ref, token_ref):
@@ -200,9 +202,11 @@
     panels = [panels[mask] for mask in range(panel_total)]
 
     half_shape = jax.ShapeDtypeStruct((item_rows // 2, rank), jnp.float32)
+    narrow = item_rows // device_total % 16 == 0
+    sent_shape = jax.ShapeDtypeStruct(half_shape.shape, jnp.bfloat16 if narrow else jnp.float32)
     keep, send, weighted, item_whole = pl.pallas_call(
         functools.partial(item_kernel, device_total, groups),
-        out_shape=(half_shape, half_shape, held, jax.ShapeDtypeStruct((item_rows, rank), jnp.bfloat16)),
+        out_shape=(half_shape, sent_shape, held, jax.ShapeDtypeStruct((item_rows, rank), jnp.bfloat16)),
         in_specs=[SMEM] * 4 + [VMEM] * (4 + panel_total),
         out_specs=(VMEM,) * 4,
         scratch_shapes=[pltpu.VMEM((item_rows // block, block, rank), jnp.float32)],

time: 34 us -> 34 us (level); the launches traced: 33.8 us -> 34.2 us
  Pallas kernels: 5.58 us -> 8.2 us
  starting transfers between devices: 17.3 us -> 15.9 us
  waiting for transfers between devices: 7.23 us -> 6.42 us
    ppermute x10, starting transfers between devices: 17.3 us -> 15.9 us  [permute(): lax.ppermute(array, AXES, [(index, index ^ mask) for index in range(devic...]
    pallas_call x1, Pallas kernels: 2.17 us -> 3.4 us  [body(): pl.pallas_call(functools.partial(item_kernel, device_total, groups), out_...]
    ppermute x10, waiting for transfers between devices: 7.23 us -> 6.42 us  [permute(): lax.ppermute(array, AXES, [(index, index ^ mask) for index in range(devic...]
    pallas_call x1, Pallas kernels: 1.44 us -> 2.2 us  [body(): pl.pallas_call(user_kernel, out_shape=(jax.ShapeDtypeStruct((user_rows, r...]
    pallas_call x1, Pallas kernels: 1.89 us -> 2.52 us  [body(): pl.pallas_call(stage_kernel, out_shape=(held, held, jax.ShapeDtypeStruct(...]
  transfers between devices with their start and end apart: 10 -> 10, of which waited for: 6 -> 6; matrix products, arithmetic and copies ran while one was open for 5% -> 5% of each run, Pallas kernels for 10% -> 14%
where the time goes in v2:
time: 34 us; the launch traced here: 34.2 us
  starting transfers between devices  15.9 us (47%)
  Pallas kernels  8.2 us (24%)
  waiting for transfers between devices  6.42 us (19%)
  other arithmetic  2.3 us (7%)
  between operations  1.35 us (4%)
    ppermute x10, starting transfers between devices, permute(): lax.ppermute(array, AXES, [(index, index ^ mask) for index in range(devic...  15.9 us
    ppermute x10, waiting for transfers between devices, permute(): lax.ppermute(array, AXES, [(index, index ^ mask) for index in range(devic...  6.42 us
    pallas_call x1, Pallas kernels, body(): pl.pallas_call(functools.partial(item_kernel, device_total, groups), out_...  3.4 us
    pallas_call x1, Pallas kernels, body(): pl.pallas_call(stage_kernel, out_shape=(held, held, jax.ShapeDtypeStruct(...  2.52 us
    pallas_call x1, Pallas kernels, body(): pl.pallas_call(user_kernel, out_shape=(jax.ShapeDtypeStruct((user_rows, r...  2.2 us
    add x1, other arithmetic, body(): user_sums * grad_scale + decay_rate * user_factors.astype(jnp.float32)  1.59 us
  transfers between devices with their start and end apart: 10, of which 6 were waited for; matrix products, arithmetic and copies ran while one was open for 5% of the time, Pallas kernels for 14%

profile of v2, /device:TPU:0, one launch (start us, length us, event | category | flops | bytes accessed | tf_op | source)
XLA Modules:
  0.0 34.2 jit_solution(2713906092601436612)
XLA Ops:
  0.6 3.0 %collective-permute-start = (bf16[256,256]{1,0:T(8,128)(2,1)}, bf16[256,256]{1,0:T(8,128)(2,1)S(1)}, u32[]{:S(2)}, u32[]{:S(2)}) collective-permute-start(bf16[256,256]{1,0:T(8,128)(2,1)} %refs_0_.1), channel_id=1, source_target_pairs={{0,2},{1,3},{2,0},{3,1},{4,6},{5,7},{6,4},{7,5},{8,10},{9,11},{10,... | collective-permute-start | bytes 393224 | tf_op jit(solution)/shard_map/ppermute | solution.py:177
  3.7 0.0 collective-permute-start.1
  4.3 0.1 pad_add_fusion.place_ref
  4.4 0.0 copy-start
  4.4 0.0 copy-start.1
  4.4 0.0 copy-start.2
  4.4 0.0 copy-start.3
  4.4 2.5 %stage.1 = (bf16[128,128,128]{2,1,0:T(8,128)(2,1)S(1)}, bf16[128,128,128]{2,1,0:T(8,128)(2,1)S(1)}, f32[8,128]{1,0:T(8,128)S(1)}) custom-call(s32[1]{0:T(128)S(6)} %copy.9.count_ref, s32[2]{0:T(128)S(1)} %pad_add_fusion.place_ref, bf16[1,128,128,128]{3,2,1,0:T(8,128)(2,1)} %rating_ref.1, bf16[1,128,128,128]{3,2,1,0:T(8,128)(2,1)} %weight_ref.1), custom_call_target="tpu_custom_call" | custom-call | bytes 18000000 | tf_op jit(solution)/shard_map/stage/pallas_call | solution.py:189
  6.9 0.4 %collective-permute-done.refs_2_ = bf16[256,256]{1,0:T(8,128)(2,1)S(1)} collective-permute-done((bf16[256,256]{1,0:T(8,128)(2,1)}, bf16[256,256]{1,0:T(8,128)(2,1)S(1)}, u32[]{:S(2)}, u32[]{:S(2)}) %collective-permute-start) | collective-permute-done | bytes 131104 | tf_op jit(solution)/shard_map/ppermute | solution.py:177
  7.4 0.0 collective-permute-start.2
  7.4 0.0 collective-permute-done.1.refs_1_
  7.4 1.3 %collective-permute-done.2.refs_3_ = bf16[256,256]{1,0:T(8,128)(2,1)S(1)} collective-permute-done((bf16[256,256]{1,0:T(8,128)(2,1)S(1)}, bf16[256,256]{1,0:T(8,128)(2,1)S(1)}, u32[]{:S(2)}, u32[]{:S(2)}) %collective-permute-start.2) | collective-permute-done | bytes 131104 | tf_op jit(solution)/shard_map/ppermute | solution.py:177
  8.7 0.0 copy-done
  8.7 0.0 copy-done.1
  8.7 0.0 copy-done.2
  8.7 0.0 copy-done.3
  8.7 3.4 %item_sums.1 = (f32[512,256]{1,0:T(8,128)S(1)}, bf16[512,256]{1,0:T(8,128)(2,1)S(1)}, bf16[128,128,128]{2,1,0:T(8,128)(2,1)S(1)}, bf16[1024,256]{1,0:T(8,128)(2,1)S(1)}) custom-call(s32[1]{0:T(128)S(6)} %copy.9.count_ref, s32[2]{0:T(128)S(1)} %pad_add_fusion.place_ref, s32[1,128]{1,0:T(1,128)S(1)} %copy-done.2, s32[1,128]{1,0:T(1,128)S(1)} %copy-done.3, ...), custom_call_target="tpu_custom_call" | custom-call | bytes 24000000 | tf_op jit(solution)/shard_map/item_sums/pallas_call | solution.py:207
  12.2 0.2 collective-permute-start.3
  12.4 1.4 %collective-permute-done.3.refs_1_ = bf16[512,256]{1,0:T(8,128)(2,1)S(1)} collective-permute-done((bf16[512,256]{1,0:T(8,128)(2,1)S(1)}, bf16[512,256]{1,0:T(8,128)(2,1)S(1)}, u32[]{:S(2)}, u32[]{:S(2)}) %collective-permute-start.3) | collective-permute-done | bytes 262176 | tf_op jit(solution)/shard_map/ppermute | solution.py:177
  13.8 2.7 %collective-permute-start.4 = (bf16[128,256]{1,0:T(8,128)(2,1)S(1)}, bf16[128,256]{1,0:T(8,128)(2,1)S(1)}, u32[]{:S(2)}, u32[]{:S(2)}) collective-permute-start(bf16[128,256]{1,0:T(8,128)(2,1)S(1)} %get-tuple-element.37), channel_id=1, source_target_pairs={{0,6},{1,7},{2,4},{3,5},{4,2},{5,3},{6,0},{7,1},{8,14},{9,15},{10,... | collective-permute-start | bytes 196616 | tf_op jit(solution)/shard_map/ppermute | solution.py:177
  16.5 2.8 %collective-permute-start.5 = (bf16[128,256]{1,0:T(8,128)(2,1)S(1)}, bf16[128,256]{1,0:T(8,128)(2,1)S(1)}, u32[]{:S(2)}, u32[]{:S(2)}) collective-permute-start(bf16[128,256]{1,0:T(8,128)(2,1)S(1)} %get-tuple-element.38), channel_id=1, source_target_pairs={{0,4},{1,5},{2,6},{3,7},{4,0},{5,1},{6,2},{7,3},{8,12},{9,13},{10,... | collective-permute-start | bytes 196616 | tf_op jit(solution)/shard_map/ppermute | solution.py:177
  19.4 1.4 %collective-permute-start.6 = (bf16[128,256]{1,0:T(8,128)(2,1)S(1)}, bf16[128,256]{1,0:T(8,128)(2,1)S(1)}, u32[]{:S(2)}, u32[]{:S(2)}) collective-permute-start(bf16[128,256]{1,0:T(8,128)(2,1)S(1)} %get-tuple-element.39), channel_id=1, source_target_pairs={{0,2},{1,3},{2,0},{3,1},{4,6},{5,7},{6,4},{7,5},{8,10},{9,11},{10,... | collective-permute-start | bytes 196616 | tf_op jit(solution)/shard_map/ppermute | solution.py:177
  20.8 2.2 %user_sums.1 = (f32[2048,256]{1,0:T(8,128)S(1)}, f32[8,128]{1,0:T(8,128)S(1)}) custom-call(s32[1]{0:T(128)S(6)} %copy.9.count_ref, s32[2]{0:T(128)S(1)} %pad_add_fusion.place_ref, s32[1,128]{1,0:T(1,128)S(1)} %copy-done.2, s32[1,128]{1,0:T(1,128)S(1)} %copy-done.3, bf16[1024,256]{1,0:T(8,128)(2,1)S(1)} %get-tuple-element.29.item_ref, ...), custom_call_target="tpu_custom_call" | custom-call | bytes 15000000 | tf_op jit(solution)/shard_map/user_sums/pallas_call | solution.py:218
  23.0 0.0 collective-permute-done.4.refs_1_
  23.0 0.3 collective-permute-done.5.refs_2_
  23.3 0.3 collective-permute-done.6.refs_3_
  23.7 5.1 %collective-permute-start.7 = (f32[32,256]{1,0:T(8,128)S(1)}, f32[32,256]{1,0:T(8,128)S(1)}, u32[]{:S(2)}, u32[]{:S(2)}) collective-permute-start(f32[32,256]{1,0:T(8,128)S(1)} %get-tuple-element.42), channel_id=1, source_target_pairs={{0,24},{1,25},{2,26},{3,27},{4,28},{5,29},{6,30},{7,31},{8,16},{9,... | collective-permute-start | bytes 98312 | tf_op jit(solution)/shard_map/ppermute | solution.py:177
  28.8 0.0 collective-permute-start.8
  28.8 0.6 %collective-permute-start.9 = (f32[32,256]{1,0:T(8,128)S(1)}, f32[32,256]{1,0:T(8,128)S(1)}, u32[]{:S(2)}, u32[]{:S(2)}) collective-permute-start(f32[32,256]{1,0:T(8,128)S(1)} %get-tuple-element.44), channel_id=1, source_target_pairs={{0,8},{1,9},{2,10},{3,11},{4,12},{5,13},{6,14},{7,15},{8,0},{9,1},... | collective-permute-start | bytes 98312 | tf_op jit(solution)/shard_map/ppermute | solution.py:177
  29.4 1.6 %multiply_add_fusion = f32[2048,256]{1,0:T(8,128)} fusion(bf16[2048,256]{1,0:T(8,128)(2,1)S(1)} %copy-done, f32[2048,256]{1,0:T(8,128)S(1)} %get-tuple-element.31), kind=kLoop, calls=%fused_computation | loop fusion | flops 2097152 | bytes 5242880 | tf_op jit(solution)/shard_map/add | solution.py:237
  31.0 0.0 collective-permute-done.7
  31.0 2.6 %collective-permute-done.8 = f32[32,256]{1,0:T(8,128)S(1)} collective-permute-done((f32[32,256]{1,0:T(8,128)S(1)}, f32[32,256]{1,0:T(8,128)S(1)}, u32[]{:S(2)}, u32[]{:S(2)}) %collective-permute-start.8) | collective-permute-done | bytes 32800 | tf_op jit(solution)/shard_map/ppermute | solution.py:177
  33.6 0.0 collective-permute-done.9
  33.6 0.6 %multiply_add_fusion.1 = f32[32,256]{1,0:T(8,128)} fusion(f32[32,256]{1,0:T(8,128)S(1)} %collective-permute-done.9, f32[32,256]{1,0:T(8,128)S(1)} %collective-permute-done.8, f32[32,256]{1,0:T(8,128)S(1)} %get-tuple-element.41, f32[32,256]{1,0:T(8,128)S(1)} %collective-permute-done.7, bf16[256,256]{1,0:T(8,128)(2,1)S(1)} %copy-done.1, s32[]{:T(128)S(6)} %select_n.27, ...), kind=kLoop, calls=%fused_computation.1 | loop fusion | flops 81920 | bytes 229383 | tf_op jit(solution)/shard_map/add | solution.py:245
  (3 shorter events, 0.1 us)
Async XLA Ops:
  0.6 6.7 %collective-permute-start = (bf16[256,256]{1,0:T(8,128)(2,1)}, bf16[256,256]{1,0:T(8,128)(2,1)S(1)}, u32[]{:S(2)}, u32[]{:S(2)}) collective-permute-start(bf16[256,256]{1,0:T(8,128)(2,1)} %refs_0_.1), channel_id=1, source_target_pairs={{0,2},{1,3},{2,0},{3,1},{4,6},{5,7},{6,4},{7,5},{8,10},{9,11},{10,... | collective-permute-start | bytes 393224 | tf_op jit(solution)/shard_map/ppermute | solution.py:177
  3.7 3.7 %collective-permute-start.1 = (bf16[256,256]{1,0:T(8,128)(2,1)}, bf16[256,256]{1,0:T(8,128)(2,1)S(1)}, u32[]{:S(2)}, u32[]{:S(2)}) collective-permute-start(bf16[256,256]{1,0:T(8,128)(2,1)} %refs_0_.1), channel_id=1, source_target_pairs={{0,1},{1,0},{2,3},{3,2},{4,5},{5,4},{6,7},{7,6},{8,9},{9,8},{10,11... | collective-permute-start | bytes 393224 | tf_op jit(solution)/shard_map/ppermute | solution.py:177
  4.4 4.3 %copy-start = (bf16[2048,256]{1,0:T(8,128)(2,1)S(1)}, bf16[2048,256]{1,0:T(8,128)(2,1)}, u32[]{:S(2)}) copy-start(bf16[2048,256]{1,0:T(8,128)(2,1)} %user_ref.1) | copy-start | bytes 3145732
  4.4 4.3 %copy-start.1 = (bf16[256,256]{1,0:T(8,128)(2,1)S(1)}, bf16[256,256]{1,0:T(8,128)(2,1)}, u32[]{:S(2)}) copy-start(bf16[256,256]{1,0:T(8,128)(2,1)} %refs_0_.1) | copy-start | bytes 393220
  4.4 4.3 %copy-start.2 = (s32[1,128]{1,0:T(1,128)S(1)}, s32[1,128]{1,0:T(1,128)}, u32[]{:S(2)}) copy-start(s32[1,128]{1,0:T(1,128)} %user_id_ref.3) | copy-start | bytes 1540
  4.4 4.3 %copy-start.3 = (s32[1,128]{1,0:T(1,128)S(1)}, s32[1,128]{1,0:T(1,128)}, u32[]{:S(2)}) copy-start(s32[1,128]{1,0:T(1,128)} %item_id_ref.3) | copy-start | bytes 1540
  7.4 1.3 %collective-permute-start.2 = (bf16[256,256]{1,0:T(8,128)(2,1)S(1)}, bf16[256,256]{1,0:T(8,128)(2,1)S(1)}, u32[]{:S(2)}, u32[]{:S(2)}) collective-permute-start(bf16[256,256]{1,0:T(8,128)(2,1)S(1)} %collective-permute-done.refs_2_), channel_id=1, source_target_pairs={{0,1},{1,0},{2,3},{3,2},{4,5},{5,4},{6,7},{7,6},{8,9},{9,8},{10,11... | collective-permute-start | bytes 393224 | tf_op jit(solution)/shard_map/ppermute | solution.py:177
  12.2 1.6 %collective-permute-start.3 = (bf16[512,256]{1,0:T(8,128)(2,1)S(1)}, bf16[512,256]{1,0:T(8,128)(2,1)S(1)}, u32[]{:S(2)}, u32[]{:S(2)}) collective-permute-start(bf16[512,256]{1,0:T(8,128)(2,1)S(1)} %get-tuple-element.34), channel_id=1, source_target_pairs={{0,1},{1,0},{2,3},{3,2},{4,5},{5,4},{6,7},{7,6},{8,9},{9,8},{10,11... | collective-permute-start | bytes 786440 | tf_op jit(solution)/shard_map/ppermute | solution.py:177
  13.8 9.2 %collective-permute-start.4 = (bf16[128,256]{1,0:T(8,128)(2,1)S(1)}, bf16[128,256]{1,0:T(8,128)(2,1)S(1)}, u32[]{:S(2)}, u32[]{:S(2)}) collective-permute-start(bf16[128,256]{1,0:T(8,128)(2,1)S(1)} %get-tuple-element.37), channel_id=1, source_target_pairs={{0,6},{1,7},{2,4},{3,5},{4,2},{5,3},{6,0},{7,1},{8,14},{9,15},{10,... | collective-permute-start | bytes 196616 | tf_op jit(solution)/shard_map/ppermute | solution.py:177
  16.5 6.8 %collective-permute-start.5 = (bf16[128,256]{1,0:T(8,128)(2,1)S(1)}, bf16[128,256]{1,0:T(8,128)(2,1)S(1)}, u32[]{:S(2)}, u32[]{:S(2)}) collective-permute-start(bf16[128,256]{1,0:T(8,128)(2,1)S(1)} %get-tuple-element.38), channel_id=1, source_target_pairs={{0,4},{1,5},{2,6},{3,7},{4,0},{5,1},{6,2},{7,3},{8,12},{9,13},{10,... | collective-permute-start | bytes 196616 | tf_op jit(solution)/shard_map/ppermute | solution.py:177
  19.4 4.3 %collective-permute-start.6 = (bf16[128,256]{1,0:T(8,128)(2,1)S(1)}, bf16[128,256]{1,0:T(8,128)(2,1)S(1)}, u32[]{:S(2)}, u32[]{:S(2)}) collective-permute-start(bf16[128,256]{1,0:T(8,128)(2,1)S(1)} %get-tuple-element.39), channel_id=1, source_target_pairs={{0,2},{1,3},{2,0},{3,1},{4,6},{5,7},{6,4},{7,5},{8,10},{9,11},{10,... | collective-permute-start | bytes 196616 | tf_op jit(solution)/shard_map/ppermute | solution.py:177
  23.7 7.3 %collective-permute-start.7 = (f32[32,256]{1,0:T(8,128)S(1)}, f32[32,256]{1,0:T(8,128)S(1)}, u32[]{:S(2)}, u32[]{:S(2)}) collective-permute-start(f32[32,256]{1,0:T(8,128)S(1)} %get-tuple-element.42), channel_id=1, source_target_pairs={{0,24},{1,25},{2,26},{3,27},{4,28},{5,29},{6,30},{7,31},{8,16},{9,... | collective-permute-start | bytes 98312 | tf_op jit(solution)/shard_map/ppermute | solution.py:177
  28.8 4.8 %collective-permute-start.8 = (f32[32,256]{1,0:T(8,128)S(1)}, f32[32,256]{1,0:T(8,128)S(1)}, u32[]{:S(2)}, u32[]{:S(2)}) collective-permute-start(f32[32,256]{1,0:T(8,128)S(1)} %get-tuple-element.43), channel_id=1, source_target_pairs={{0,16},{1,17},{2,18},{3,19},{4,20},{5,21},{6,22},{7,23},{8,24},{9,... | collective-permute-start | bytes 98312 | tf_op jit(solution)/shard_map/ppermute | solution.py:177
  28.8 4.8 %collective-permute-start.9 = (f32[32,256]{1,0:T(8,128)S(1)}, f32[32,256]{1,0:T(8,128)S(1)}, u32[]{:S(2)}, u32[]{:S(2)}) collective-permute-start(f32[32,256]{1,0:T(8,128)S(1)} %get-tuple-element.44), channel_id=1, source_target_pairs={{0,8},{1,9},{2,10},{3,11},{4,12},{5,13},{6,14},{7,15},{8,0},{9,1},... | collective-permute-start | bytes 98312 | tf_op jit(solution)/shard_map/ppermute | solution.py:177

commit v3 on v2

--- a/solution.py
+++ b/solution.py
@@ -98,7 +98,7 @@
         return carry
 
     lax.fori_loop(0, turns, turn, 0)
-    own_place = place_ref[0]
+    own_place = place_of(place_ref[0], groups)
     owned = keep_ref.shape[0] * 2 // owner_total
     half = owner_total // 2
     per_block = block // owned
@@ -182,7 +182,7 @@
             cost_estimate=pl.CostEstimate(flops=0, bytes_accessed=int(3e6 * micros), transcendentals=0),
         )
 
-    places = jnp.stack([place_of(me, groups), panel_index * (panel_rows // block)]).astype(jnp.int32)
+    places = jnp.stack([me, panel_index * (panel_rows // block)]).astype(jnp.int32)
     held = jax.ShapeDtypeStruct((slots, block, block), jnp.bfloat16)
     sems = pltpu.SemaphoreType.DMA((turns,))
     direct = {mask: permute(item_factors, mask) for mask in [*range(2, panel_total, 2), 1]}

time: 34 us -> 33.4 us (0.982); the launches traced: 34.2 us -> 33.1 us
  Pallas kernels: 8.2 us -> 13.6 us
  starting transfers between devices: 15.9 us -> 11.2 us
  waiting for transfers between devices: 6.42 us -> 4.63 us
    ppermute x10, starting transfers between devices: 15.9 us -> 11.2 us  [permute(): lax.ppermute(array, AXES, [(index, index ^ mask) for index in range(devic...]
    pallas_call x1, Pallas kernels: 3.4 us -> 6.02 us  [body(): pl.pallas_call(functools.partial(item_kernel, device_total, groups), out_...]
    ppermute x10, waiting for transfers between devices: 6.42 us -> 4.63 us  [permute(): lax.ppermute(array, AXES, [(index, index ^ mask) for index in range(devic...]
    pallas_call x1, Pallas kernels: 2.2 us -> 3.71 us  [body(): pl.pallas_call(user_kernel, out_shape=(jax.ShapeDtypeStruct((user_rows, r...]
    pallas_call x1, Pallas kernels: 2.52 us -> 3.76 us  [body(): pl.pallas_call(stage_kernel, out_shape=(held, held, jax.ShapeDtypeStruct(...]
  transfers between devices with their start and end apart: 10 -> 10, of which waited for: 6 -> 4; matrix products, arithmetic and copies ran while one was open for 5% -> 5% of each run, Pallas kernels for 14% -> 23%
where the time goes in v3:
time: 33.4 us; the launch traced here: 33.1 us
  Pallas kernels  13.6 us (41%)
  starting transfers between devices  11.2 us (34%)
  waiting for transfers between devices  4.63 us (14%)
  other arithmetic  2.3 us (7%)
  between operations  1.39 us (4%)
    ppermute x10, starting transfers between devices, permute(): lax.ppermute(array, AXES, [(index, index ^ mask) for index in range(devic...  11.2 us
    pallas_call x1, Pallas kernels, body(): pl.pallas_call(functools.partial(item_kernel, device_total, groups), out_...  6.02 us
    ppermute x10, waiting for transfers between devices, permute(): lax.ppermute(array, AXES, [(index, index ^ mask) for index in range(devic...  4.63 us
    pallas_call x1, Pallas kernels, body(): pl.pallas_call(stage_kernel, out_shape=(held, held, jax.ShapeDtypeStruct(...  3.76 us
    pallas_call x1, Pallas kernels, body(): pl.pallas_call(user_kernel, out_shape=(jax.ShapeDtypeStruct((user_rows, r...  3.71 us
    add x1, other arithmetic, body(): user_sums * grad_scale + decay_rate * user_factors.astype(jnp.float32)  1.59 us
  transfers between devices with their start and end apart: 10, of which 4 were waited for; matrix products, arithmetic and copies ran while one was open for 5% of the time, Pallas kernels for 23%

profile of v3, /device:TPU:0, one launch (start us, length us, event | category | flops | bytes accessed | tf_op | source)
XLA Modules:
  0.0 33.1 jit_solution(13371327379390196565)
XLA Ops:
  0.6 3.0 %collective-permute-start = (bf16[256,256]{1,0:T(8,128)(2,1)}, bf16[256,256]{1,0:T(8,128)(2,1)S(1)}, u32[]{:S(2)}, u32[]{:S(2)}) collective-permute-start(bf16[256,256]{1,0:T(8,128)(2,1)} %refs_0_.1), channel_id=1, source_target_pairs={{0,2},{1,3},{2,0},{3,1},{4,6},{5,7},{6,4},{7,5},{8,10},{9,11},{10,... | collective-permute-start | bytes 393224 | tf_op jit(solution)/shard_map/ppermute | solution.py:177
  3.7 0.0 collective-permute-start.1
  4.3 0.1 pad_add_fusion.place_ref
  4.4 0.0 copy-start
  4.4 0.0 copy-start.1
  4.4 0.0 copy-start.2
  4.4 0.0 copy-start.3
  4.4 3.8 %stage.1 = (bf16[128,128,128]{2,1,0:T(8,128)(2,1)S(1)}, bf16[128,128,128]{2,1,0:T(8,128)(2,1)S(1)}, f32[8,128]{1,0:T(8,128)S(1)}) custom-call(s32[1]{0:T(128)S(6)} %copy.9.count_ref, s32[2]{0:T(128)S(1)} %pad_add_fusion.place_ref, bf16[1,128,128,128]{3,2,1,0:T(8,128)(2,1)} %rating_ref.1, bf16[1,128,128,128]{3,2,1,0:T(8,128)(2,1)} %weight_ref.1), custom_call_target="tpu_custom_call" | custom-call | bytes 18000000 | tf_op jit(solution)/shard_map/stage/pallas_call | solution.py:189
  8.2 0.0 collective-permute-done.refs_2_
  8.2 0.1 collective-permute-start.2
  8.3 0.0 collective-permute-done.1.refs_1_
  8.3 1.3 %collective-permute-done.2.refs_3_ = bf16[256,256]{1,0:T(8,128)(2,1)S(1)} collective-permute-done((bf16[256,256]{1,0:T(8,128)(2,1)S(1)}, bf16[256,256]{1,0:T(8,128)(2,1)S(1)}, u32[]{:S(2)}, u32[]{:S(2)}) %collective-permute-start.2) | collective-permute-done | bytes 131104 | tf_op jit(solution)/shard_map/ppermute | solution.py:177
  9.6 0.0 copy-done
  9.6 0.0 copy-done.1
  9.6 0.0 copy-done.2
  9.6 0.0 copy-done.3
  9.6 6.0 %item_sums.1 = (f32[512,256]{1,0:T(8,128)S(1)}, bf16[512,256]{1,0:T(8,128)(2,1)S(1)}, bf16[128,128,128]{2,1,0:T(8,128)(2,1)S(1)}, bf16[1024,256]{1,0:T(8,128)(2,1)S(1)}) custom-call(s32[1]{0:T(128)S(6)} %copy.9.count_ref, s32[2]{0:T(128)S(1)} %pad_add_fusion.place_ref, s32[1,128]{1,0:T(1,128)S(1)} %copy-done.2, s32[1,128]{1,0:T(1,128)S(1)} %copy-done.3, ...), custom_call_target="tpu_custom_call" | custom-call | bytes 24000000 | tf_op jit(solution)/shard_map/item_sums/pallas_call | solution.py:207
  15.6 0.1 collective-permute-start.3
  15.7 1.5 %collective-permute-done.3.refs_1_ = bf16[512,256]{1,0:T(8,128)(2,1)S(1)} collective-permute-done((bf16[512,256]{1,0:T(8,128)(2,1)S(1)}, bf16[512,256]{1,0:T(8,128)(2,1)S(1)}, u32[]{:S(2)}, u32[]{:S(2)}) %collective-permute-start.3) | collective-permute-done | bytes 262176 | tf_op jit(solution)/shard_map/ppermute | solution.py:177
  17.3 1.9 %collective-permute-start.4 = (bf16[128,256]{1,0:T(8,128)(2,1)S(1)}, bf16[128,256]{1,0:T(8,128)(2,1)S(1)}, u32[]{:S(2)}, u32[]{:S(2)}) collective-permute-start(bf16[128,256]{1,0:T(8,128)(2,1)S(1)} %get-tuple-element.37), channel_id=1, source_target_pairs={{0,6},{1,7},{2,4},{3,5},{4,2},{5,3},{6,0},{7,1},{8,14},{9,15},{10,... | collective-permute-start | bytes 196616 | tf_op jit(solution)/shard_map/ppermute | solution.py:177
  19.2 0.5 %collective-permute-start.5 = (bf16[128,256]{1,0:T(8,128)(2,1)S(1)}, bf16[128,256]{1,0:T(8,128)(2,1)S(1)}, u32[]{:S(2)}, u32[]{:S(2)}) collective-permute-start(bf16[128,256]{1,0:T(8,128)(2,1)S(1)} %get-tuple-element.38), channel_id=1, source_target_pairs={{0,4},{1,5},{2,6},{3,7},{4,0},{5,1},{6,2},{7,3},{8,12},{9,13},{10,... | collective-permute-start | bytes 196616 | tf_op jit(solution)/shard_map/ppermute | solution.py:177
  19.7 1.2 %collective-permute-start.6 = (bf16[128,256]{1,0:T(8,128)(2,1)S(1)}, bf16[128,256]{1,0:T(8,128)(2,1)S(1)}, u32[]{:S(2)}, u32[]{:S(2)}) collective-permute-start(bf16[128,256]{1,0:T(8,128)(2,1)S(1)} %get-tuple-element.39), channel_id=1, source_target_pairs={{0,2},{1,3},{2,0},{3,1},{4,6},{5,7},{6,4},{7,5},{8,10},{9,11},{10,... | collective-permute-start | bytes 196616 | tf_op jit(solution)/shard_map/ppermute | solution.py:177
  20.9 3.7 %user_sums.1 = (f32[2048,256]{1,0:T(8,128)S(1)}, f32[8,128]{1,0:T(8,128)S(1)}) custom-call(s32[1]{0:T(128)S(6)} %copy.9.count_ref, s32[2]{0:T(128)S(1)} %pad_add_fusion.place_ref, s32[1,128]{1,0:T(1,128)S(1)} %copy-done.2, s32[1,128]{1,0:T(1,128)S(1)} %copy-done.3, bf16[1024,256]{1,0:T(8,128)(2,1)S(1)} %get-tuple-element.29.item_ref, ...), custom_call_target="tpu_custom_call" | custom-call | bytes 15000000 | tf_op jit(solution)/shard_map/user_sums/pallas_call | solution.py:218
  24.6 0.0 collective-permute-done.4.refs_1_
  24.6 0.0 collective-permute-done.5.refs_2_
  24.6 0.0 collective-permute-done.6.refs_3_
  24.6 2.7 %collective-permute-start.7 = (f32[32,256]{1,0:T(8,128)S(1)}, f32[32,256]{1,0:T(8,128)S(1)}, u32[]{:S(2)}, u32[]{:S(2)}) collective-permute-start(f32[32,256]{1,0:T(8,128)S(1)} %get-tuple-element.42), channel_id=1, source_target_pairs={{0,24},{1,25},{2,26},{3,27},{4,28},{5,29},{6,30},{7,31},{8,16},{9,... | collective-permute-start | bytes 98312 | tf_op jit(solution)/shard_map/ppermute | solution.py:177
  27.3 0.9 %collective-permute-start.8 = (f32[32,256]{1,0:T(8,128)S(1)}, f32[32,256]{1,0:T(8,128)S(1)}, u32[]{:S(2)}, u32[]{:S(2)}) collective-permute-start(f32[32,256]{1,0:T(8,128)S(1)} %get-tuple-element.43), channel_id=1, source_target_pairs={{0,16},{1,17},{2,18},{3,19},{4,20},{5,21},{6,22},{7,23},{8,24},{9,... | collective-permute-start | bytes 98312 | tf_op jit(solution)/shard_map/ppermute | solution.py:177
  28.2 0.9 %collective-permute-start.9 = (f32[32,256]{1,0:T(8,128)S(1)}, f32[32,256]{1,0:T(8,128)S(1)}, u32[]{:S(2)}, u32[]{:S(2)}) collective-permute-start(f32[32,256]{1,0:T(8,128)S(1)} %get-tuple-element.44), channel_id=1, source_target_pairs={{0,8},{1,9},{2,10},{3,11},{4,12},{5,13},{6,14},{7,15},{8,0},{9,1},... | collective-permute-start | bytes 98312 | tf_op jit(solution)/shard_map/ppermute | solution.py:177
  29.1 1.6 %multiply_add_fusion = f32[2048,256]{1,0:T(8,128)} fusion(bf16[2048,256]{1,0:T(8,128)(2,1)S(1)} %copy-done, f32[2048,256]{1,0:T(8,128)S(1)} %get-tuple-element.31), kind=kLoop, calls=%fused_computation | loop fusion | flops 2097152 | bytes 5242880 | tf_op jit(solution)/shard_map/add | solution.py:237
  30.7 0.0 collective-permute-done.7
  30.7 1.5 %collective-permute-done.8 = f32[32,256]{1,0:T(8,128)S(1)} collective-permute-done((f32[32,256]{1,0:T(8,128)S(1)}, f32[32,256]{1,0:T(8,128)S(1)}, u32[]{:S(2)}, u32[]{:S(2)}) %collective-permute-start.8) | collective-permute-done | bytes 32800 | tf_op jit(solution)/shard_map/ppermute | solution.py:177
  32.2 0.2 collective-permute-done.9
  32.5 0.6 %multiply_add_fusion.1 = f32[32,256]{1,0:T(8,128)} fusion(f32[32,256]{1,0:T(8,128)S(1)} %collective-permute-done.9, f32[32,256]{1,0:T(8,128)S(1)} %collective-permute-done.8, f32[32,256]{1,0:T(8,128)S(1)} %get-tuple-element.41, f32[32,256]{1,0:T(8,128)S(1)} %collective-permute-done.7, bf16[256,256]{1,0:T(8,128)(2,1)S(1)} %copy-done.1, s32[]{:T(128)S(6)} %select_n.27, ...), kind=kLoop, calls=%fused_computation.1 | loop fusion | flops 81920 | bytes 229383 | tf_op jit(solution)/shard_map/add | solution.py:245
  (3 shorter events, 0.1 us)
Async XLA Ops:
  0.6 7.5 %collective-permute-start = (bf16[256,256]{1,0:T(8,128)(2,1)}, bf16[256,256]{1,0:T(8,128)(2,1)S(1)}, u32[]{:S(2)}, u32[]{:S(2)}) collective-permute-start(bf16[256,256]{1,0:T(8,128)(2,1)} %refs_0_.1), channel_id=1, source_target_pairs={{0,2},{1,3},{2,0},{3,1},{4,6},{5,7},{6,4},{7,5},{8,10},{9,11},{10,... | collective-permute-start | bytes 393224 | tf_op jit(solution)/shard_map/ppermute | solution.py:177
  3.7 4.6 %collective-permute-start.1 = (bf16[256,256]{1,0:T(8,128)(2,1)}, bf16[256,256]{1,0:T(8,128)(2,1)S(1)}, u32[]{:S(2)}, u32[]{:S(2)}) collective-permute-start(bf16[256,256]{1,0:T(8,128)(2,1)} %refs_0_.1), channel_id=1, source_target_pairs={{0,1},{1,0},{2,3},{3,2},{4,5},{5,4},{6,7},{7,6},{8,9},{9,8},{10,11... | collective-permute-start | bytes 393224 | tf_op jit(solution)/shard_map/ppermute | solution.py:177
  4.4 5.2 %copy-start = (bf16[2048,256]{1,0:T(8,128)(2,1)S(1)}, bf16[2048,256]{1,0:T(8,128)(2,1)}, u32[]{:S(2)}) copy-start(bf16[2048,256]{1,0:T(8,128)(2,1)} %user_ref.1) | copy-start | bytes 3145732
  4.4 5.2 %copy-start.1 = (bf16[256,256]{1,0:T(8,128)(2,1)S(1)}, bf16[256,256]{1,0:T(8,128)(2,1)}, u32[]{:S(2)}) copy-start(bf16[256,256]{1,0:T(8,128)(2,1)} %refs_0_.1) | copy-start | bytes 393220
  4.4 5.2 %copy-start.2 = (s32[1,128]{1,0:T(1,128)S(1)}, s32[1,128]{1,0:T(1,128)}, u32[]{:S(2)}) copy-start(s32[1,128]{1,0:T(1,128)} %user_id_ref.3) | copy-start | bytes 1540
  4.4 5.2 %copy-start.3 = (s32[1,128]{1,0:T(1,128)S(1)}, s32[1,128]{1,0:T(1,128)}, u32[]{:S(2)}) copy-start(s32[1,128]{1,0:T(1,128)} %item_id_ref.3) | copy-start | bytes 1540
  8.2 1.4 %collective-permute-start.2 = (bf16[256,256]{1,0:T(8,128)(2,1)S(1)}, bf16[256,256]{1,0:T(8,128)(2,1)S(1)}, u32[]{:S(2)}, u32[]{:S(2)}) collective-permute-start(bf16[256,256]{1,0:T(8,128)(2,1)S(1)} %collective-permute-done.refs_2_), channel_id=1, source_target_pairs={{0,1},{1,0},{2,3},{3,2},{4,5},{5,4},{6,7},{7,6},{8,9},{9,8},{10,11... | collective-permute-start | bytes 393224 | tf_op jit(solution)/shard_map/ppermute | solution.py:177
  15.6 1.6 %collective-permute-start.3 = (bf16[512,256]{1,0:T(8,128)(2,1)S(1)}, bf16[512,256]{1,0:T(8,128)(2,1)S(1)}, u32[]{:S(2)}, u32[]{:S(2)}) collective-permute-start(bf16[512,256]{1,0:T(8,128)(2,1)S(1)} %get-tuple-element.34), channel_id=1, source_target_pairs={{0,1},{1,0},{2,3},{3,2},{4,5},{5,4},{6,7},{7,6},{8,9},{9,8},{10,11... | collective-permute-start | bytes 786440 | tf_op jit(solution)/shard_map/ppermute | solution.py:177
  17.3 7.3 %collective-permute-start.4 = (bf16[128,256]{1,0:T(8,128)(2,1)S(1)}, bf16[128,256]{1,0:T(8,128)(2,1)S(1)}, u32[]{:S(2)}, u32[]{:S(2)}) collective-permute-start(bf16[128,256]{1,0:T(8,128)(2,1)S(1)} %get-tuple-element.37), channel_id=1, source_target_pairs={{0,6},{1,7},{2,4},{3,5},{4,2},{5,3},{6,0},{7,1},{8,14},{9,15},{10,... | collective-permute-start | bytes 196616 | tf_op jit(solution)/shard_map/ppermute | solution.py:177
  19.2 5.4 %collective-permute-start.5 = (bf16[128,256]{1,0:T(8,128)(2,1)S(1)}, bf16[128,256]{1,0:T(8,128)(2,1)S(1)}, u32[]{:S(2)}, u32[]{:S(2)}) collective-permute-start(bf16[128,256]{1,0:T(8,128)(2,1)S(1)} %get-tuple-element.38), channel_id=1, source_target_pairs={{0,4},{1,5},{2,6},{3,7},{4,0},{5,1},{6,2},{7,3},{8,12},{9,13},{10,... | collective-permute-start | bytes 196616 | tf_op jit(solution)/shard_map/ppermute | solution.py:177
  19.7 4.9 %collective-permute-start.6 = (bf16[128,256]{1,0:T(8,128)(2,1)S(1)}, bf16[128,256]{1,0:T(8,128)(2,1)S(1)}, u32[]{:S(2)}, u32[]{:S(2)}) collective-permute-start(bf16[128,256]{1,0:T(8,128)(2,1)S(1)} %get-tuple-element.39), channel_id=1, source_target_pairs={{0,2},{1,3},{2,0},{3,1},{4,6},{5,7},{6,4},{7,5},{8,10},{9,11},{10,... | collective-permute-start | bytes 196616 | tf_op jit(solution)/shard_map/ppermute | solution.py:177
  24.6 6.0 %collective-permute-start.7 = (f32[32,256]{1,0:T(8,128)S(1)}, f32[32,256]{1,0:T(8,128)S(1)}, u32[]{:S(2)}, u32[]{:S(2)}) collective-permute-start(f32[32,256]{1,0:T(8,128)S(1)} %get-tuple-element.42), channel_id=1, source_target_pairs={{0,24},{1,25},{2,26},{3,27},{4,28},{5,29},{6,30},{7,31},{8,16},{9,... | collective-permute-start | bytes 98312 | tf_op jit(solution)/shard_map/ppermute | solution.py:177
  27.3 4.9 %collective-permute-start.8 = (f32[32,256]{1,0:T(8,128)S(1)}, f32[32,256]{1,0:T(8,128)S(1)}, u32[]{:S(2)}, u32[]{:S(2)}) collective-permute-start(f32[32,256]{1,0:T(8,128)S(1)} %get-tuple-element.43), channel_id=1, source_target_pairs={{0,16},{1,17},{2,18},{3,19},{4,20},{5,21},{6,22},{7,23},{8,24},{9,... | collective-permute-start | bytes 98312 | tf_op jit(solution)/shard_map/ppermute | solution.py:177
  28.2 4.3 %collective-permute-start.9 = (f32[32,256]{1,0:T(8,128)S(1)}, f32[32,256]{1,0:T(8,128)S(1)}, u32[]{:S(2)}, u32[]{:S(2)}) collective-permute-start(f32[32,256]{1,0:T(8,128)S(1)} %get-tuple-element.44), channel_id=1, source_target_pairs={{0,8},{1,9},{2,10},{3,11},{4,12},{5,13},{6,14},{7,15},{8,0},{9,1},... | collective-permute-start | bytes 98312 | tf_op jit(solution)/shard_map/ppermute | solution.py:177
